TPU v7x, 256 devices: a whole 4x4x8 slice. The times are simulated.
256 devices in a mesh: line: 16 (over z, x_hi), seg: 16 (over y, x_lo, core).
Axes of the slice: x: 4 (x_hi: 2, x_lo: 2; x = x_hi * 2 + x_lo), y: 4, z: 8, core: 2. Of those that a mesh axis runs over, the one named last changes fastest.
Arguments:
- feats: float32 [16, 32768, 512], P('line', 'seg'), as said below
- norm_gain: float32 [512], replicated, may hold values from 0.1 to 1.9
- w_qkv: float32 [512, 1536], replicated, as said below
- w_out: float32 [512, 512], replicated, may hold values from -0.25 to 0.25
- counts: int32 [16, 256], P('line', 'seg'), may hold values from 1 to 128
- partner: int32 [16, 16], P('line', 'seg'), may hold values from 0 to 1, as said below
- cross_list: int32 [16, 256, 2], P('line', 'seg'), may hold values from -1 to 15, as said below
Outputs:
- mixed: float32 [16, 32768, 512], P('line', 'seg')
Inputs may be any that keep to these rules, and one draw needn't show every extreme that they name: partner of the first line is 1 and of the last line is 0. `cross_list`: the entries of a row that are not -1 are distinct. `w_qkv`: entries have magnitude under 4. `feats`: entries have magnitude under 60.
All inputs are finite; a program needn't handle non-finite values.
Results may differ from a plain program's by a relative error of at most 0.0003.
Values sent between devices are 32-bit elements; how exact they have to be, the bound alone decides.
A program may use at most 192 MiB of HBM per device.

v0:
```python
import jax
import jax.numpy as jnp
from jax import lax
from jax.sharding import PartitionSpec as P

HEADS = 8
BLK = 128


def shifted(block, axis, distance):
    devices = range(lax.axis_size(axis))
    route = [(i - distance, i) for i in devices if i - distance in devices]
    return lax.ppermute(block, axis, route)


def layer_norm(values, gain):
    center = values - jnp.mean(values, axis=-1, keepdims=True)
    spread = jnp.mean(center * center, axis=-1, keepdims=True)
    return center * lax.rsqrt(spread + 1e-05) * gain


def attend_blocks(queries, key_vals, key_mask, width):
    head_size = width // HEADS
    groups = queries.shape[0]
    q_heads = queries.reshape(groups, BLK, HEADS, head_size)
    k_heads = key_vals[..., :width].reshape(groups, -1, HEADS, head_size)
    v_heads = key_vals[..., width:].reshape(groups, -1, HEADS, head_size)
    scores = jnp.einsum(
        "bqhd,bkhd->bhqk", q_heads, k_heads, precision=lax.Precision.HIGHEST
    ) * head_size ** (-0.5)
    scores = jnp.where(key_mask[:, None, None, :], scores, -1e30)
    top = jnp.max(scores, axis=-1, keepdims=True)
    weights = jnp.where(key_mask[:, None, None, :], jnp.exp(scores - top), 0.0)
    total = jnp.sum(weights, axis=-1)
    summed = jnp.einsum("bhqk,bkhd->bqhd", weights, v_heads, precision=lax.Precision.HIGHEST)
    summed = summed / jnp.transpose(total, (0, 2, 1))[..., None]
    return summed.reshape(groups * BLK, width)


def body(feats, norm_gain, w_qkv, w_out, counts, partner, cross_list):
    points = feats[0]
    block_counts = counts[0]
    rows = points.shape[0]
    width = points.shape[1]
    blocks = block_counts.shape[0]
    w_kv = w_qkv[:, width:]
    normed = layer_norm(points, norm_gain)
    queries = jnp.dot(normed, w_qkv[:, :width], precision=lax.Precision.HIGHEST)
    own_kv = jnp.dot(normed, w_kv, precision=lax.Precision.HIGHEST)
    prev_rows, prev_count = shifted((own_kv[rows - BLK :], block_counts[blocks - 1 :]), "seg", 1)
    next_rows, next_count = shifted((own_kv[:BLK], block_counts[:1]), "seg", -1)
    below_rows, below_count = shifted((own_kv, block_counts), "line", 1)
    above_rows, above_count = shifted((own_kv, block_counts), "line", -1)
    upward = partner[0, 0] == 1
    strip_rows = jnp.where(upward, above_rows, below_rows)
    strip_count = jnp.where(upward, above_count, below_count)
    ext_kv = jnp.concatenate([prev_rows, own_kv, next_rows], axis=0)
    ext_count = jnp.concatenate([prev_count, block_counts, next_count], axis=0)
    offsets = jnp.arange(BLK, dtype=jnp.int32)
    ext_blocks = ext_kv.reshape(blocks + 2, BLK, 2 * width)
    ext_live = offsets[None, :] < ext_count[:, None]
    strip_blocks = strip_rows.reshape(blocks, BLK, 2 * width)
    strip_live = offsets[None, :] < strip_count[:, None]
    listed_all = cross_list[0]
    group = min(4, blocks)

    def attend_group(group_index):
        start = group_index * group
        local_kv = jnp.stack(
            [lax.dynamic_slice_in_dim(ext_blocks, start + offset, group, 0) for offset in range(3)],
            axis=1,
        )
        local_live = jnp.stack(
            [lax.dynamic_slice_in_dim(ext_live, start + offset, group, 0) for offset in range(3)],
            axis=1,
        )
        listed = lax.dynamic_slice_in_dim(listed_all, start, group, 0)
        picked = jnp.maximum(listed, 0)
        cross_kv = strip_blocks[picked]
        cross_live = strip_live[picked] & (listed >= 0)[:, :, None]
        all_kv = jnp.concatenate([local_kv, cross_kv], axis=1).reshape(group, -1, 2 * width)
        all_live = jnp.concatenate([local_live, cross_live], axis=1).reshape(group, -1)
        group_q = lax.dynamic_slice_in_dim(queries, start * BLK, group * BLK, 0).reshape(
            group, BLK, width
        )
        return attend_blocks(group_q, all_kv, all_live, width)

    attended = lax.map(attend_group, jnp.arange(blocks // group, dtype=jnp.int32)).reshape(
        rows, width
    )
    result = points + jnp.dot(attended, w_out, precision=lax.Precision.HIGHEST)
    row_live = (offsets[None, :] < block_counts[:, None]).reshape(rows)
    return jnp.where(row_live[:, None], result, 0.0)[None]


def solution(mesh):
    in_specs = (
        P("line", "seg", None),
        P(),
        P(),
        P(),
        P("line", "seg"),
        P("line", "seg"),
        P("line", "seg", None),
    )
    out_specs = P("line", "seg", None)
    return jax.shard_map(body, mesh=mesh, in_specs=in_specs, out_specs=out_specs, check_vma=False)
```

profile of v0, /device:TPU:8, one launch (start us, length us, event | category | flops | bytes accessed | tf_op | source)
XLA Modules:
  0.0 803.4 jit_solution(11929495493700529403)
XLA Ops:
  6.1 17.6 %fusion.23 = f32[2048,1024]{1,0:T(8,128)} fusion(f32[1,2048,512]{2,1,0:T(8,128)S(1)} %copy-done.2, f32[512,1536]{1,0:T(8,128)} %param.11, f32[512]{0:T(512)S(1)} %copy-done.3, f32[2048]{0:T(1024)S(1)} %add_rsqrt_fusion, f32[2048]{0:T(1024)S(1)} %broadcast_multiply_fusion), kind=kOutput, calls=%fused_computation.49 | convolution fusion | flops 12888047616 | bytes 14698496 | tf_op jit(solution)/shard_map/dot_general | solution.py:49
  25.0 9.3 %collective-permute-start.3 = (f32[2048,1024]{1,0:T(8,128)}, f32[2048,1024]{1,0:T(8,128)}, u32[]{:S(2)}, u32[]{:S(2)}) collective-permute-start(f32[2048,1024]{1,0:T(8,128)} %fusion.23), channel_id=1, source_target_pairs={{0,16},{16,32},{32,48},{48,64},{64,80},{80,96},{96,112},{112,128},... | collective-permute-start | bytes 25165832 | tf_op jit(solution)/shard_map/ppermute | solution.py:13
  44.7 11.2 %fusion.22 = f32[2048,512]{0,1:T(8,128)} fusion(f32[1,2048,512]{2,1,0:T(8,128)} %param.9, f32[512]{0:T(512)S(1)} %copy-done.3, f32[2048]{0:T(1024)S(1)} %add_rsqrt_fusion, f32[2048]{0:T(1024)S(1)} %broadcast_multiply_fusion, f32[512,1536]{1,0:T(8,128)} %param.11), kind=kOutput, calls=%fused_computation.48 | convolution fusion | flops 6445596672 | bytes 9455616 | tf_op jit(solution)/shard_map/dot_general | solution.py:48
  55.8 340.2 %collective-permute-done.4 = s32[1]{0:T(128)} collective-permute-done((s32[1]{0:T(128)}, s32[1]{0:T(128)}, u32[]{:S(2)}, u32[]{:S(2)}) %collective-permute-start.4) | collective-permute-done | bytes 36 | tf_op jit(solution)/shard_map/ppermute | solution.py:13
  410.5 8.9 %pad_maximum_fusion.1 = f32[2304,1024]{1,0:T(8,128)} fusion(f32[128,1024]{1,0:T(8,128)S(1)} %collective-permute-done.1, f32[2048,1024]{1,0:T(8,128)} %fusion.23, f32[128,1024]{1,0:T(8,128)S(1)} %collective-permute-done), kind=kLoop, calls=%fused_computation.40 | loop fusion | flops 4718592 | bytes 18874368 | tf_op jit(solution)/shard_map/concatenate | solution.py:57
  419.5 9.7 %broadcast_select_fusion = f32[2048,1024]{1,0:T(8,128)} fusion(f32[2048,1024]{1,0:T(8,128)} %collective-permute-done.2, f32[2048,1024]{1,0:T(8,128)} %collective-permute-done.3, pred[]{:T(512)} %bitcast.5), kind=kLoop, calls=%fused_computation.47 | loop fusion | flops 2097152 | bytes 25165824 | tf_op jit(solution)/shard_map/jit(_where)/select_n | solution.py:55
  429.2 363.6 %while.13 = (s32[]{:T(128)}, f32[4,512,512]{2,1,0:T(8,128)}, s32[4]{0:T(128)S(1)}, f32[18,128,1024]{2,1,0:T(8,128)}, s32[16,2]{0,1:T(2,128)S(1)}, /*index=5*/f32...) while((s32[]{:T(128)}, f32[4,512,512]{2,1,0:T(8,128)}, ...), condition=%wide.region_5.6_spmd.clone, body=%wide.region_2.5_spmd.clone.sunk | while | flops 4066119168 | bytes 180474800 | solution.py:88
  443.2 6.0 dynamic-slice_bitcast_fusion.4
  449.5 6.3 gather_fusion
  455.8 9.4 %pad_maximum_fusion.3 = f32[4,5,128,1024]{3,2,1,0:T(8,128)} fusion(f32[4,2,128,1024]{3,2,1,0:T(8,128)} %bitcast.97, f32[4,1,128,1024]{3,2,1,0:T(8,128)} %get-tuple-element.266, f32[4,1,128,1024]{3,2,1,0:T(8,128)} %get-tuple-element.267, f32[4,1,128,1024]{3,2,1,0:T(8,128)S(1)} %get-tuple-element.268), kind=kLoop, calls=%fused_computation.3.clone.1 | loop fusion | flops 7864320 | bytes 20971520 | tf_op jit(solution)/shard_map/while/body/eval_jaxpr/concatenate | solution.py:81
  465.2 9.2 %fusion.49 = (f32[4,640,512]{2,1,0:T(8,128)}, f32[4,640,512]{2,1,0:T(8,128)}) fusion(f32[4,640,1024]{2,1,0:T(8,128)} %bitcast.95), kind=kLoop, calls=%fused_computation.65.clone.1 | loop fusion | bytes 20971520 | tf_op jit(solution)/shard_map/while/body/eval_jaxpr/slice | solution.py:26
  483.5 12.0 %fusion.51 = (f32[4,8,128]{2,1,0:T(8,128)S(1)}, f32[4,8,128,640]{3,2,1,0:T(8,128)S(1)}) fusion(pred[4,640]{1,0:T(4,128)(4,1)S(1)} %bitcast.102, f32[4,640,8,64]{1,3,2,0:T(8,128)} %bitcast.96, f32[4,128,8,64]{1,0,3,2:T(4,128)S(1)} %reshape.128), kind=kOutput, calls=%fused_computation.6.clone.1 | convolution fusion | flops 2021126144 | bytes 16796160 | tf_op jit(solution)/shard_map/while/body/eval_jaxpr/bqhd,bkhd->bhqk/dot_general | solution.py:28
  499.4 5.9 copy.62
  505.3 18.7 %fusion.53 = f32[4,128,8,64]{1,3,2,0:T(8,128)} fusion(f32[4,640,8,64]{1,3,2,0:T(8,128)} %bitcast.99, f32[4,8,128,640]{3,2,1,0:T(8,128)} %copy-done.1, f32[4,8,128]{2,1,0:T(8,128)S(1)} %get-tuple-element.275, pred[4,640]{1,0:T(4,128)(4,1)S(1)} %bitcast.104, f32[4,128,8]{1,2,0:T(8,128)S(1)} %bitcast.105), kind=kOutput, calls=%fused_computation.20.clone.1 | convolution fusion | flops 2024013824 | bytes 16812544 | tf_op jit(solution)/shard_map/while/body/eval_jaxpr/bhqk,bkhd->bqhd/dot_general | solution.py:35
  531.1 5.9 dynamic-slice_bitcast_fusion.4
  537.3 6.3 gather_fusion
  543.5 9.4 %pad_maximum_fusion.3 = f32[4,5,128,1024]{3,2,1,0:T(8,128)} fusion(f32[4,2,128,1024]{3,2,1,0:T(8,128)} %bitcast.97, f32[4,1,128,1024]{3,2,1,0:T(8,128)} %get-tuple-element.266, f32[4,1,128,1024]{3,2,1,0:T(8,128)} %get-tuple-element.267, f32[4,1,128,1024]{3,2,1,0:T(8,128)S(1)} %get-tuple-element.268), kind=kLoop, calls=%fused_computation.3.clone.1 | loop fusion | flops 7864320 | bytes 20971520 | tf_op jit(solution)/shard_map/while/body/eval_jaxpr/concatenate | solution.py:81
  553.0 9.2 %fusion.49 = (f32[4,640,512]{2,1,0:T(8,128)}, f32[4,640,512]{2,1,0:T(8,128)}) fusion(f32[4,640,1024]{2,1,0:T(8,128)} %bitcast.95), kind=kLoop, calls=%fused_computation.65.clone.1 | loop fusion | bytes 20971520 | tf_op jit(solution)/shard_map/while/body/eval_jaxpr/slice | solution.py:26
  571.2 12.0 %fusion.51 = (f32[4,8,128]{2,1,0:T(8,128)S(1)}, f32[4,8,128,640]{3,2,1,0:T(8,128)S(1)}) fusion(pred[4,640]{1,0:T(4,128)(4,1)S(1)} %bitcast.102, f32[4,640,8,64]{1,3,2,0:T(8,128)} %bitcast.96, f32[4,128,8,64]{1,0,3,2:T(4,128)S(1)} %reshape.128), kind=kOutput, calls=%fused_computation.6.clone.1 | convolution fusion | flops 2021126144 | bytes 16796160 | tf_op jit(solution)/shard_map/while/body/eval_jaxpr/bqhd,bkhd->bhqk/dot_general | solution.py:28
  587.2 5.9 copy.62
  593.1 18.7 %fusion.53 = f32[4,128,8,64]{1,3,2,0:T(8,128)} fusion(f32[4,640,8,64]{1,3,2,0:T(8,128)} %bitcast.99, f32[4,8,128,640]{3,2,1,0:T(8,128)} %copy-done.1, f32[4,8,128]{2,1,0:T(8,128)S(1)} %get-tuple-element.275, pred[4,640]{1,0:T(4,128)(4,1)S(1)} %bitcast.104, f32[4,128,8]{1,2,0:T(8,128)S(1)} %bitcast.105), kind=kOutput, calls=%fused_computation.20.clone.1 | convolution fusion | flops 2024013824 | bytes 16812544 | tf_op jit(solution)/shard_map/while/body/eval_jaxpr/bhqk,bkhd->bqhd/dot_general | solution.py:35
  624.9 6.3 gather_fusion
  631.2 9.4 %pad_maximum_fusion.3 = f32[4,5,128,1024]{3,2,1,0:T(8,128)} fusion(f32[4,2,128,1024]{3,2,1,0:T(8,128)} %bitcast.97, f32[4,1,128,1024]{3,2,1,0:T(8,128)} %get-tuple-element.266, f32[4,1,128,1024]{3,2,1,0:T(8,128)} %get-tuple-element.267, f32[4,1,128,1024]{3,2,1,0:T(8,128)S(1)} %get-tuple-element.268), kind=kLoop, calls=%fused_computation.3.clone.1 | loop fusion | flops 7864320 | bytes 20971520 | tf_op jit(solution)/shard_map/while/body/eval_jaxpr/concatenate | solution.py:81
  640.6 9.2 %fusion.49 = (f32[4,640,512]{2,1,0:T(8,128)}, f32[4,640,512]{2,1,0:T(8,128)}) fusion(f32[4,640,1024]{2,1,0:T(8,128)} %bitcast.95), kind=kLoop, calls=%fused_computation.65.clone.1 | loop fusion | bytes 20971520 | tf_op jit(solution)/shard_map/while/body/eval_jaxpr/slice | solution.py:26
  658.9 12.0 %fusion.51 = (f32[4,8,128]{2,1,0:T(8,128)S(1)}, f32[4,8,128,640]{3,2,1,0:T(8,128)S(1)}) fusion(pred[4,640]{1,0:T(4,128)(4,1)S(1)} %bitcast.102, f32[4,640,8,64]{1,3,2,0:T(8,128)} %bitcast.96, f32[4,128,8,64]{1,0,3,2:T(4,128)S(1)} %reshape.128), kind=kOutput, calls=%fused_computation.6.clone.1 | convolution fusion | flops 2021126144 | bytes 16796160 | tf_op jit(solution)/shard_map/while/body/eval_jaxpr/bqhd,bkhd->bhqk/dot_general | solution.py:28
  680.7 18.7 %fusion.53 = f32[4,128,8,64]{1,3,2,0:T(8,128)} fusion(f32[4,640,8,64]{1,3,2,0:T(8,128)} %bitcast.99, f32[4,8,128,640]{3,2,1,0:T(8,128)} %copy-done.1, f32[4,8,128]{2,1,0:T(8,128)S(1)} %get-tuple-element.275, pred[4,640]{1,0:T(4,128)(4,1)S(1)} %bitcast.104, f32[4,128,8]{1,2,0:T(8,128)S(1)} %bitcast.105), kind=kOutput, calls=%fused_computation.20.clone.1 | convolution fusion | flops 2024013824 | bytes 16812544 | tf_op jit(solution)/shard_map/while/body/eval_jaxpr/bhqk,bkhd->bqhd/dot_general | solution.py:35
  712.6 6.3 gather_fusion
  718.8 9.4 %pad_maximum_fusion.3 = f32[4,5,128,1024]{3,2,1,0:T(8,128)} fusion(f32[4,2,128,1024]{3,2,1,0:T(8,128)} %bitcast.97, f32[4,1,128,1024]{3,2,1,0:T(8,128)} %get-tuple-element.266, f32[4,1,128,1024]{3,2,1,0:T(8,128)} %get-tuple-element.267, f32[4,1,128,1024]{3,2,1,0:T(8,128)S(1)} %get-tuple-element.268), kind=kLoop, calls=%fused_computation.3.clone.1 | loop fusion | flops 7864320 | bytes 20971520 | tf_op jit(solution)/shard_map/while/body/eval_jaxpr/concatenate | solution.py:81
  728.3 9.2 %fusion.49 = (f32[4,640,512]{2,1,0:T(8,128)}, f32[4,640,512]{2,1,0:T(8,128)}) fusion(f32[4,640,1024]{2,1,0:T(8,128)} %bitcast.95), kind=kLoop, calls=%fused_computation.65.clone.1 | loop fusion | bytes 20971520 | tf_op jit(solution)/shard_map/while/body/eval_jaxpr/slice | solution.py:26
  746.5 12.0 %fusion.51 = (f32[4,8,128]{2,1,0:T(8,128)S(1)}, f32[4,8,128,640]{3,2,1,0:T(8,128)S(1)}) fusion(pred[4,640]{1,0:T(4,128)(4,1)S(1)} %bitcast.102, f32[4,640,8,64]{1,3,2,0:T(8,128)} %bitcast.96, f32[4,128,8,64]{1,0,3,2:T(4,128)S(1)} %reshape.128), kind=kOutput, calls=%fused_computation.6.clone.1 | convolution fusion | flops 2021126144 | bytes 16796160 | tf_op jit(solution)/shard_map/while/body/eval_jaxpr/bqhd,bkhd->bhqk/dot_general | solution.py:28
  768.4 18.7 %fusion.53 = f32[4,128,8,64]{1,3,2,0:T(8,128)} fusion(f32[4,640,8,64]{1,3,2,0:T(8,128)} %bitcast.99, f32[4,8,128,640]{3,2,1,0:T(8,128)} %copy-done.1, f32[4,8,128]{2,1,0:T(8,128)S(1)} %get-tuple-element.275, pred[4,640]{1,0:T(4,128)(4,1)S(1)} %bitcast.104, f32[4,128,8]{1,2,0:T(8,128)S(1)} %bitcast.105), kind=kOutput, calls=%fused_computation.20.clone.1 | convolution fusion | flops 2024013824 | bytes 16812544 | tf_op jit(solution)/shard_map/while/body/eval_jaxpr/bhqk,bkhd->bqhd/dot_general | solution.py:35
  792.8 10.4 %fusion.21 = f32[1,2048,512]{2,1,0:T(8,128)} fusion(f32[1,2048,512]{2,1,0:T(8,128)} %param.9, f32[2048,512]{1,0:T(8,128)} %bitcast.101, f32[512,512]{1,0:T(8,128)S(1)} %copy-done, pred[2048]{0:T(1024)(128)(4,1)S(1)} %copy-done.5), kind=kOutput, calls=%fused_computation.44 | convolution fusion | flops 6444548096 | bytes 13633536 | tf_op jit(solution)/shard_map/dot_general | solution.py:91
  (146 shorter events, 130.5 us)
Async XLA Ops:
  0.0 792.8 %copy-start = (f32[512,512]{1,0:T(8,128)S(1)}, f32[512,512]{1,0:T(8,128)}, u32[]{:S(2)}) copy-start(f32[512,512]{1,0:T(8,128)} %param.12) | copy-start | bytes 3145732
  0.0 5.7 copy-start.3
  2.6 3.5 copy-start.2
  6.1 31.5 %copy-start.6 = (s32[1,16]{1,0:T(1,128)S(1)}, s32[1,16]{1,0:T(1,128)}, u32[]{:S(2)}) copy-start(s32[1,16]{1,0:T(1,128)} %param.13) | copy-start | bytes 196
  23.7 395.7 %collective-permute-start.2 = (f32[2048,1024]{1,0:T(8,128)}, f32[2048,1024]{1,0:T(8,128)}, u32[]{:S(2)}, u32[]{:S(2)}) collective-permute-start(f32[2048,1024]{1,0:T(8,128)} %fusion.23), channel_id=1, source_target_pairs={{16,0},{32,16},{48,32},{64,48},{80,64},{96,80},{112,96},{128,112},... | collective-permute-start | bytes 25165832 | tf_op jit(solution)/shard_map/ppermute | solution.py:13
  25.0 394.4 %collective-permute-start.3 = (f32[2048,1024]{1,0:T(8,128)}, f32[2048,1024]{1,0:T(8,128)}, u32[]{:S(2)}, u32[]{:S(2)}) collective-permute-start(f32[2048,1024]{1,0:T(8,128)} %fusion.23), channel_id=1, source_target_pairs={{0,16},{16,32},{32,48},{48,64},{64,80},{80,96},{96,112},{112,128},... | collective-permute-start | bytes 25165832 | tf_op jit(solution)/shard_map/ppermute | solution.py:13
  35.6 374.9 %collective-permute-start = (f32[128,1024]{1,0:T(8,128)S(1)}, f32[128,1024]{1,0:T(8,128)S(1)}, u32[]{:S(2)}, u32[]{:S(2)}) collective-permute-start(f32[128,1024]{1,0:T(8,128)S(1)} %get-tuple-element.197), channel_id=1, source_target_pairs={{0,1},{1,2},{2,3},{3,4},{4,5},{5,6},{6,7},{7,8},{8,9},{9,10},{10,1... | collective-permute-start | bytes 1572872 | tf_op jit(solution)/shard_map/ppermute | solution.py:13
  37.6 367.5 %collective-permute-start.6 = (s32[16]{0:T(128)S(1)}, s32[16]{0:T(128)S(1)}, u32[]{:S(2)}, u32[]{:S(2)}) collective-permute-start(s32[16]{0:T(128)S(1)} %bitcast.107), channel_id=1, source_target_pairs={{16,0},{32,16},{48,32},{64,48},{80,64},{96,80},{112,96},{128,112},... | collective-permute-start | bytes 200 | tf_op jit(solution)/shard_map/ppermute | solution.py:13
  39.5 356.5 %collective-permute-start.4 = (s32[1]{0:T(128)}, s32[1]{0:T(128)}, u32[]{:S(2)}, u32[]{:S(2)}) collective-permute-start(s32[1]{0:T(128)} %bitcast.7), channel_id=1, source_target_pairs={{0,1},{1,2},{2,3},{3,4},{4,5},{5,6},{6,7},{7,8},{8,9},{9,10},{10,1... | collective-permute-start | bytes 20 | tf_op jit(solution)/shard_map/ppermute | solution.py:13
  396.0 3.4 collective-permute-start.5
  399.4 11.2 %collective-permute-start.1 = (f32[128,1024]{1,0:T(8,128)S(1)}, f32[128,1024]{1,0:T(8,128)S(1)}, u32[]{:S(2)}, u32[]{:S(2)}) collective-permute-start(f32[128,1024]{1,0:T(8,128)S(1)} %get-tuple-element.198), channel_id=1, source_target_pairs={{1,0},{2,1},{3,2},{4,3},{5,4},{6,5},{7,6},{8,7},{9,8},{10,9},{11,1... | collective-permute-start | bytes 1572872 | tf_op jit(solution)/shard_map/ppermute | solution.py:13
  405.0 5.5 collective-permute-start.7
  419.5 9.7 %copy-start.4 = (s32[1,16,2]{1,2,0:T(2,128)S(1)}, s32[1,16,2]{1,2,0:T(2,128)}, u32[]{:S(2)}) copy-start(s32[1,16,2]{1,2,0:T(2,128)} %param.15) | copy-start | bytes 388
  429.2 363.6 %copy-start.5 = (pred[2048]{0:T(1024)(128)(4,1)S(1)}, pred[2048]{0:T(1024)(128)(4,1)}, u32[]{:S(2)}) copy-start(pred[2048]{0:T(1024)(128)(4,1)} %fusion.32) | copy-start | bytes 6148
  495.4 4.0 copy-start.1
  583.2 4.0 copy-start.1
  670.8 4.0 copy-start.1
  758.5 4.0 copy-start.1
where the time goes:
time: 815 us; the launch traced here: 803 us
  waiting for transfers between devices  346 us (42%)
  local copies, waits for them, and re-layouts  175 us (21%)
  matrix products  162 us (20%)
  other arithmetic  75.9 us (9%)
  starting transfers between devices  25.3 us (3%)
  loops' own time  18.6 us (2%)
    ppermute x8, waiting for transfers between devices, shifted(): return lax.ppermute(block, axis, route)  346 us
    dot_general x4, matrix products, attend_blocks(): jnp.einsum('bhqk,bkhd->bqhd', weights, v_heads, precision=lax.Precision.H...  75 us
    slice x8, local copies, waits for them, and re-layouts, attend_blocks(): k_heads = key_vals[..., :width].reshape(groups, -1, HEADS, head_size)  60.2 us
    dot_general x4, matrix products, attend_blocks(): jnp.einsum('bqhd,bkhd->bhqk', q_heads, k_heads, precision=lax.Precision.H...  47.8 us
    concatenate x4, other arithmetic, attend_group(): jnp.concatenate([local_kv, cross_kv], axis=1).reshape(group, -1, 2 * width)  37.7 us
    ppermute x8, starting transfers between devices, shifted(): return lax.ppermute(block, axis, route)  25.3 us
    gather x4, local copies, waits for them, and re-layouts, attend_group(): cross_kv = strip_blocks[picked]  25 us
    slice x4, local copies, waits for them, and re-layouts, attend_blocks(): v_heads = key_vals[..., width:].reshape(groups, -1, HEADS, head_size)  23.6 us
  transfers between devices with their start and end apart: 8, of which 3 were waited for; matrix products, arithmetic and copies ran while one was open for 3% of the time, Pallas kernels for 0%

commit v1 on v0

v1 whole, which is shorter than its diff:
```python
import functools
import math

import jax
import jax.numpy as jnp
from jax import lax
from jax.experimental import pallas as pl
from jax.experimental.pallas import tpu as pltpu
from jax.sharding import PartitionSpec as P

MESH = pl.DeviceIdType.MESH
F32, BF16 = jnp.float32, jnp.bfloat16
HEADS = 8
BLK = 128
DIM = 64
PAIR = 2 * DIM
RING = 8
MASKED = -1e30
NT = (((1,), (1,)), ((), ()))


def split(x):
    high = x.astype(BF16)
    return high, (x - high.astype(F32)).astype(BF16)


def dot(a, b):
    return jnp.dot(a, b, preferred_element_type=F32)


def dot3(ah, al, bh, bl):
    return dot(ah, bh) + dot(al, bh) + dot(ah, bl)


def normalize(x):
    center = x - jnp.mean(x, axis=-1, keepdims=True)
    spread = jnp.mean(center * center, axis=-1, keepdims=True)
    return center * lax.rsqrt(spread + 1e-05)


def iota(shape, dim):
    return lax.broadcasted_iota(jnp.int32, shape, dim)


def swap(x):
    return pltpu.roll(x, DIM, 1)


def kernel(
    blocks,
    feats, gain, w_qkv, w_out, counts, counts_row, partner, listed,
    out,
    own, near, far, halo, cnt,
    w_hi, w_lo, q_all, k_ring, v_ring, k_strip, v_strip, mixed, lse_all,
    x_send, x_recv, z_send, z_recv, h_send, h_recv, c_send, c_recv,
    own_sem, w_sem, out_sem,
):
    groups = blocks // 2
    rows = 2 * BLK
    width = own.shape[1]
    pairs = width // PAIR
    line, seg = lax.axis_index("line"), lax.axis_index("seg")
    lines, segs = lax.axis_size("line"), lax.axis_size("seg")
    odd = lax.rem(line, 2)
    mate = line + 1 - 2 * odd
    ahead = lax.rem(line + 2 - 4 * odd + lines, lines)
    behind = lax.rem(line - 2 + 4 * odd + lines, lines)
    right, left = lax.rem(seg + 1, segs), lax.rem(seg + segs - 1, segs)

    def group_rows(i):
        return pl.ds(pl.multiple_of(i * rows, rows), rows)

    def block_rows(b):
        return pl.ds(pl.multiple_of(b * BLK, BLK), BLK)

    def own_copy(i):
        return pltpu.make_async_copy(feats.at[group_rows(i)], own.at[group_rows(i)], own_sem.at[i])

    def w_copy(j):
        source = w_out if j == 3 else w_qkv.at[:, pl.ds(j * width, width)]
        return pltpu.make_async_copy(source, mixed.at[pl.ds(j * width, width)], w_sem.at[j])

    def out_copy(i):
        return pltpu.make_async_copy(mixed.at[group_rows(i)], out.at[group_rows(i)], out_sem.at[i])

    def remote(source, target, send, recv, device):
        return pltpu.make_async_remote_copy(
            src_ref=source, dst_ref=target, send_sem=send, recv_sem=recv,
            device_id=device, device_id_type=MESH,
        )

    def x_copy(c):
        return remote(feats.at[block_rows(c)], near.at[block_rows(c)], x_send.at[c], x_recv.at[c], (mate, seg))

    def z_copy(c):
        return remote(near.at[block_rows(c)], far.at[block_rows(c)], z_send.at[c], z_recv.at[c], (ahead, seg))

    def h_copy(j):
        b, device = ((blocks - 1), (line, right)) if j == 0 else (0, (line, left))
        return remote(feats.at[pl.ds(b * BLK, BLK)], halo.at[pl.ds(j * BLK, BLK)], h_send.at[j], h_recv.at[j], device)

    def c_copy(j):
        source = cnt.at[2] if j == 3 else counts_row
        device = ((line, right), (line, left), (mate, seg), (ahead, seg))[j]
        return remote(source, cnt.at[j], c_send.at[j], c_recv.at[j], device)

    barrier = pltpu.get_barrier_semaphore()
    for device in ((mate, seg), (ahead, seg), (behind, seg), (line, right), (line, left)):
        pl.semaphore_signal(barrier, inc=1, device_id=device, device_id_type=MESH)
    for j in range(4):
        w_copy(j).start()
    for i in range(groups):
        own_copy(i).start()
    pl.semaphore_wait(barrier, 5)
    for j in range(3):
        c_copy(j).start()
    for j in range(2):
        h_copy(j).start()

    @pl.loop(0, blocks)
    def _(c):
        x_copy(c).start()

    for j in range(4):
        w_copy(j).wait()
        w = mixed[j * width : (j + 1) * width]
        if j < 3:
            w = w * gain[...]
        if j == 0:
            w = w * (DIM**-0.5 * math.log2(math.e))
        w_hi[:, j * width : (j + 1) * width], w_lo[:, j * width : (j + 1) * width] = split(w)

    def low(n):
        return iota((n, PAIR), 1) < DIM

    def mark(n):
        return iota((n, PAIR), 1) == DIM

    def weights(j, p):
        columns = pl.ds(j * width + p * 2 * PAIR, 2 * PAIR)
        return w_hi[:, columns], w_lo[:, columns]

    def bias_of(count):
        dead = (iota((BLK, PAIR), 0) >= count) & mark(BLK)
        return jnp.where(dead, MASKED, 0.0)

    def count_in(row, b):
        return jnp.sum(jnp.where(iota(row.shape, 1) == b, row, 0.0), axis=1, keepdims=True).astype(jnp.int32)

    def store_keys(xh, xl, k_ref, v_ref, slots, bias):
        lo = low(rows)
        for p in range(pairs // 2):
            both = dot3(xh, xl, *weights(1, p))
            for half in range(2):
                h = 4 * p + 2 * half
                k = both[:, half * PAIR : (half + 1) * PAIR]
                kh = k.astype(BF16).astype(F32)
                kl = k - kh
                kh_, kl_ = swap(kh), swap(kl)
                for head, a, b in ((h, jnp.where(lo, kh, kl_), kh), (h + 1, jnp.where(lo, kh_, kl), kh_)):
                    a = a.astype(BF16)
                    b = jnp.where(lo, b, bias).astype(BF16)
                    for n, slot in enumerate(slots):
                        k_ref[slot, head, :, :PAIR] = a[n * BLK : (n + 1) * BLK]
                        k_ref[slot, head, :, PAIR:] = b[n * BLK : (n + 1) * BLK]
        for p in range(pairs // 2):
            both = dot3(xh, xl, *weights(2, p))
            for half in range(2):
                h = 4 * p + 2 * half
                v = both[:, half * PAIR : (half + 1) * PAIR]
                vh = v.astype(BF16).astype(F32)
                vl = v - vh
                for head, a in ((h, jnp.where(lo, vh, swap(vl))), (h + 1, jnp.where(lo, swap(vh), vl))):
                    a = a.astype(BF16)
                    for n, slot in enumerate(slots):
                        v_ref[slot, head] = a[n * BLK : (n + 1) * BLK]

    def own_group(i):
        own_copy(i).wait()
        xh, xl = split(normalize(own[group_rows(i)]))
        for p in range(pairs // 2):
            q_all[group_rows(i), p * 2 * PAIR : (p + 1) * 2 * PAIR] = dot3(xh, xl, *weights(0, p))
        bias = jnp.concatenate([bias_of(counts[0, 2 * i]), bias_of(counts[0, 2 * i + 1])], axis=0)
        slot = lax.rem(2 * i, RING)
        store_keys(xh, xl, k_ring, v_ring, (slot, slot + 1), bias)

    def halo_group():
        for j in range(2):
            h_copy(j).wait()
            c_copy(j).wait()
        xh, xl = split(normalize(halo[...]))
        before = jnp.where(seg == 0, 0, count_in(cnt[0, 0:1], blocks - 1))
        after = jnp.where(seg == segs - 1, 0, count_in(cnt[1, 0:1], 0))
        bias = jnp.concatenate([bias_of(before), bias_of(after)], axis=0)
        store_keys(xh, xl, k_ring, v_ring, (RING - 1, RING), bias)

    use_near = lax.rem(partner[0, 0] + odd, 2) == 1

    def strip_group(i):
        z_copy(2 * i).wait_recv()
        z_copy(2 * i + 1).wait_recv()
        x = jnp.where(use_near, near[group_rows(i)], far[group_rows(i)])
        row = jnp.where(use_near, cnt[2, 0:1], cnt[3, 0:1])
        xh, xl = split(normalize(x))
        bias = jnp.concatenate([bias_of(count_in(row, 2 * i)), bias_of(count_in(row, 2 * i + 1))], axis=0)
        store_keys(xh, xl, k_strip, v_strip, (2 * i, 2 * i + 1), bias)

    def queries(r, p):
        q = q_all[r, p * PAIR : (p + 1) * PAIR]
        lo = low(BLK)
        one = jnp.where(mark(BLK), 1.0, 0.0)
        qh = q.astype(BF16).astype(F32)
        ql = q - qh
        qh_, ql_ = swap(qh), swap(ql)
        first = jnp.concatenate([jnp.where(lo, qh, qh_), jnp.where(lo, ql, one)], axis=1).astype(BF16)
        second = jnp.concatenate([jnp.where(lo, qh_, qh), jnp.where(lo, ql_, one)], axis=1).astype(BF16)
        return first, second

    def weigh(s, top, v):
        e = jnp.exp2(s - top)
        eh, el = split(e)
        summed = dot(jnp.concatenate([eh, el], axis=0), v)
        summed = summed[:BLK] + summed[BLK:]
        return summed + swap(summed), jnp.sum(e, axis=1, keepdims=True)

    def local_block(b, slots):
        r = block_rows(b)
        lo = low(BLK)
        for p in range(pairs):
            results = []
            for n, q in enumerate(queries(r, p)):
                h = 2 * p + n
                k = jnp.concatenate([k_ring[slot, h] for slot in slots], axis=0)
                v = jnp.concatenate([v_ring[slot, h] for slot in slots], axis=0)
                s = lax.dot_general(q, k, NT, preferred_element_type=F32)
                top = jnp.max(s, axis=1, keepdims=True)
                summed, total = weigh(s, top, v)
                results.append((summed / total, jnp.broadcast_to(top + jnp.log2(total), (BLK, PAIR))))
            columns = slice(p * PAIR, (p + 1) * PAIR)
            mixed[r, columns] = jnp.where(lo, results[0][0], results[1][0])
            lse_all[r, columns] = jnp.where(lo, results[0][1], results[1][1])

    def local_group(i, last=False):
        for n in range(2):
            b = 2 * i + n
            slots = [lax.rem(b - 1 + j + RING, RING) for j in range(3)]
            if last and n == 1:
                slots[2] = RING
            local_block(b, slots)

    for h in range(HEADS):
        k_strip[blocks, h, :, :PAIR] = jnp.zeros((BLK, PAIR), BF16)
        k_strip[blocks, h, :, PAIR:] = bias_of(0).astype(BF16)
        v_strip[blocks, h] = jnp.zeros((BLK, PAIR), BF16)

    @pl.loop(0, groups)
    def _(i):
        x_copy(2 * i).wait_recv()
        z_copy(2 * i).start()

        @pl.when(i == 0)
        def _():
            c_copy(2).wait()
            c_copy(3).start()

        own_group(i)
        x_copy(2 * i + 1).wait_recv()
        z_copy(2 * i + 1).start()

        @pl.when(i == 0)
        def _():
            halo_group()
            c_copy(3).wait()

        @pl.when(i > 0)
        def _():
            local_group(i - 1)
            strip_group(i - 1)

    local_group(groups - 1, last=True)
    strip_group(groups - 1)

    @pl.loop(0, groups)
    def _(i):
        lo = low(BLK)
        attended = []
        for n in range(2):
            b = 2 * i + n
            r = block_rows(b)
            picks = [jnp.where(listed[b, j] < 0, blocks, listed[b, j]) for j in range(2)]
            tiles = []
            for p in range(pairs):
                columns = slice(p * PAIR, (p + 1) * PAIR)
                before = mixed[r, columns]
                lse_pair = lse_all[r, columns]
                results = []
                for m, q in enumerate(queries(r, p)):
                    h = 2 * p + m
                    k = jnp.concatenate([k_strip[pick, h] for pick in picks], axis=0)
                    v = jnp.concatenate([v_strip[pick, h] for pick in picks], axis=0)
                    s = lax.dot_general(q, k, NT, preferred_element_type=F32)
                    lse = lse_pair[:, m * DIM : m * DIM + 1]
                    top = jnp.maximum(jnp.max(s, axis=1, keepdims=True), lse)
                    summed, total = weigh(s, top, v)
                    weight = jnp.exp2(lse - top)
                    results.append((before * weight + summed) / (total + weight))
                tiles.append(jnp.where(lo, results[0], results[1]))
            attended.append(jnp.concatenate(tiles, axis=1))
        ah, al = split(jnp.concatenate(attended, axis=0))
        r = group_rows(i)
        row = iota((BLK, 2 * PAIR), 0)
        live = jnp.concatenate([row < counts[0, 2 * i + n] for n in range(2)], axis=0)
        for p in range(pairs // 2):
            columns = slice(p * 2 * PAIR, (p + 1) * 2 * PAIR)
            result = own[r, columns] + dot3(ah, al, *weights(3, p))
            mixed[r, columns] = jnp.where(live, result, 0.0)
        out_copy(i).start()

    @pl.loop(0, blocks)
    def _(c):
        x_copy(c).wait_send()
        z_copy(c).wait_send()

    for i in range(groups):
        out_copy(i).wait()


def body(feats, norm_gain, w_qkv, w_out, counts, partner, cross_list):
    points = feats[0]
    rows, width = points.shape
    blocks = counts.shape[1]
    groups = blocks // 2
    counts_row = jnp.zeros((8, BLK), F32).at[0, :blocks].set(counts[0].astype(F32))
    hbm = pl.BlockSpec(memory_space=pl.ANY)
    vmem = pl.BlockSpec(memory_space=pltpu.VMEM)
    smem = pl.BlockSpec(memory_space=pltpu.SMEM)
    dma = pltpu.SemaphoreType.DMA
    mixed = pl.pallas_call(
        functools.partial(kernel, blocks),
        out_shape=jax.ShapeDtypeStruct((rows, width), F32),
        in_specs=[hbm, vmem, hbm, hbm, smem, vmem, smem, smem],
        out_specs=hbm,
        scratch_shapes=[
            pltpu.VMEM((rows, width), F32),
            pltpu.VMEM((rows, width), F32),
            pltpu.VMEM((rows, width), F32),
            pltpu.VMEM((2 * BLK, width), F32),
            pltpu.VMEM((4, 8, BLK), F32),
            pltpu.VMEM((width, 4 * width), BF16),
            pltpu.VMEM((width, 4 * width), BF16),
            pltpu.VMEM((rows, width), F32),
            pltpu.VMEM((RING + 1, HEADS, BLK, 2 * PAIR), BF16),
            pltpu.VMEM((RING + 1, HEADS, BLK, PAIR), BF16),
            pltpu.VMEM((blocks + 1, HEADS, BLK, 2 * PAIR), BF16),
            pltpu.VMEM((blocks + 1, HEADS, BLK, PAIR), BF16),
            pltpu.VMEM((rows, width), F32),
            pltpu.VMEM((rows, width), F32),
            dma((blocks,)), dma((blocks,)), dma((blocks,)), dma((blocks,)),
            dma((2,)), dma((2,)), dma((4,)), dma((4,)),
            dma((groups,)), dma((4,)), dma((groups,)),
        ],
        compiler_params=pltpu.CompilerParams(
            collective_id=0, has_side_effects=True, vmem_limit_bytes=60 * 1024 * 1024
        ),
    )(points, norm_gain.reshape(width, 1), w_qkv, w_out, counts, counts_row, partner, cross_list[0])
    return mixed[None]


def solution(mesh):
    in_specs = (
        P("line", "seg", None),
        P(),
        P(),
        P(),
        P("line", "seg"),
        P("line", "seg"),
        P("line", "seg", None),
    )
    out_specs = P("line", "seg", None)
    return jax.shard_map(body, mesh=mesh, in_specs=in_specs, out_specs=out_specs, check_vma=False)
```

time: 815 us -> 186 us (0.23); the launches traced: 803 us -> 186 us
  waiting for transfers between devices: 346 us -> 0 us
  Pallas kernels: 0 us -> 177 us
  local copies, waits for them, and re-layouts: 175 us -> 8.12 us
  matrix products: 162 us -> 0 us
  other arithmetic: 75.9 us -> 0.66 us
  starting transfers between devices: 25.3 us -> 0 us
  loops' own time: 18.6 us -> 0 us
    ppermute x8 -> x0, waiting for transfers between devices: 346 us -> none  [shifted(): return lax.ppermute(block, axis, route)]
    pallas_call x0 -> x1, Pallas kernels: none -> 177 us  [body(): pl.pallas_call(functools.partial(kernel, blocks), out_shape=jax.ShapeDtyp...]
    dot_general x11 -> x0, matrix products: 162 us -> none  [the longest x4 75 us: attend_blocks(): jnp.einsum('bhqk,bkhd->bqhd', weights, v_heads, precision=lax.Precision.H...]
    slice x14 -> x0, local copies, waits for them, and re-layouts: 85.7 us -> none  [the longest x8 60.2 us: attend_blocks(): k_heads = key_vals[..., :width].reshape(groups, -1, HEADS, head_size)]
    concatenate x6 -> x0, other arithmetic: 47.9 us -> none  [the longest x4 37.7 us: attend_group(): jnp.concatenate([local_kv, cross_kv], axis=1).reshape(group, -1, 2 * width)]
    gather x12 -> x0, local copies, waits for them, and re-layouts: 27.4 us -> none  [the longest x4 25 us: attend_group(): cross_kv = strip_blocks[picked]]
    ppermute x8 -> x0, starting transfers between devices: 25.3 us -> none  [shifted(): return lax.ppermute(block, axis, route)]
    another operation x20 -> x0, local copies, waits for them, and re-layouts: 23.7 us -> none  [the longest x4 23.5 us: attend_group(): jnp.stack([lax.dynamic_slice_in_dim(ext_blocks, start + offset, group, 0)...]
  transfers between devices with their start and end apart: 8 -> 0, of which waited for: 3 -> 0; matrix products, arithmetic and copies ran while one was open for 3% -> 0% of each run, Pallas kernels for 0% -> 0%
where the time goes in v1:
time: 186 us
  Pallas kernels  177 us (95%)
  local copies, waits for them, and re-layouts  8.12 us (4%)
    pallas_call x1, Pallas kernels, body(): pl.pallas_call(functools.partial(kernel, blocks), out_shape=jax.ShapeDtyp...  177 us
    unnamed x1, local copies, waits for them, and re-layouts  4.64 us

profile of v1, /device:TPU:8, one launch (start us, length us, event | category | flops | bytes accessed | tf_op | source)
XLA Modules:
  0.0 186.1 jit_solution(17741733917343722111)
XLA Ops:
  0.7 0.7 convert_element_type.4
  1.3 0.6 scatter.4.counts_row
  1.9 1.3 copy.10.listed
  3.3 1.5 copy.9.gain
  4.8 176.6 %shard_map.73 = f32[2048,512]{1,0:T(8,128)} custom-call(f32[2048,512]{1,0:T(8,128)} %bitcast.5, f32[512,1]{1,0:T(8,128)} %copy.9.gain, f32[512,1536]{1,0:T(8,128)} %w_qkv.1, f32[512,512]{1,0:T(8,128)} %w_out.1, s32[1,16]{1,0:T(1,128)} %counts.1, f32[8,128]{1,0:T(8,128)} %scatter.4.counts_row, s32[1,1]{1,0:T(1,128)S(6)} %copy.12.partner, s32[16,2]{1,0:T(8,128)} %copy.10.listed), custom_call_target="tpu_custom_call" | custom-call | tf_op jit(solution)/shard_map/pallas_call | solution.py:338
  181.4 4.6 %copy.13 = f32[1,2048,512]{2,1,0:T(8,128)} copy(f32[1,2048,512]{2,1,0:T(8,128)} %bitcast.4) | data formatting | bytes 8388608

commit v2 on v1

v2 whole, which is shorter than its diff:
```python
import functools
import math

import jax
import jax.numpy as jnp
from jax import lax
from jax.experimental import pallas as pl
from jax.experimental.pallas import tpu as pltpu
from jax.sharding import PartitionSpec as P

MESH = pl.DeviceIdType.MESH
F32, BF16 = jnp.float32, jnp.bfloat16
HEADS = 8
BLK = 128
DIM = 64
PAIR = 2 * DIM
RING = 8
MASKED = -1e30
NT = (((1,), (1,)), ((), ()))


def split(x):
    high = x.astype(BF16)
    return high, (x - high.astype(F32)).astype(BF16)


def dot(a, b):
    return jnp.dot(a, b, preferred_element_type=F32)


def dot3(ah, al, bh, bl):
    return dot(ah, bh) + dot(al, bh) + dot(ah, bl)


def normalize(x, gain):
    center = x - jnp.mean(x, axis=-1, keepdims=True)
    spread = jnp.mean(center * center, axis=-1, keepdims=True)
    return center * lax.rsqrt(spread + 1e-05) * gain


def iota(shape, dim):
    return lax.broadcasted_iota(jnp.int32, shape, dim)


def dot_nt(a, b):
    return lax.dot_general(a, b, NT, preferred_element_type=F32)


def swap(x):
    return pltpu.roll(x, DIM, 1)


def kernel(
    blocks,
    feats, gain, w_qkv, w_out, counts, partner, listed,
    out,
    own, near, far, halo, counts_row, cnt,
    w_hi, w_lo, q_hi, q_lo, k_ring, v_ring, k_strip, v_strip, summed, tops, totals,
    x_send, x_recv, z_send, z_recv, h_send, h_recv, c_send, c_recv,
    own_sem, w_sem, out_sem,
):
    groups = blocks // 2
    rows = 2 * BLK
    width = own.shape[1]
    pairs = width // PAIR
    line, seg = lax.axis_index("line"), lax.axis_index("seg")
    lines, segs = lax.axis_size("line"), lax.axis_size("seg")
    odd = lax.rem(line, 2)
    mate = line + 1 - 2 * odd
    ahead = lax.rem(line + 2 - 4 * odd + lines, lines)
    behind = lax.rem(line - 2 + 4 * odd + lines, lines)
    right, left = lax.rem(seg + 1, segs), lax.rem(seg + segs - 1, segs)

    def group_rows(i):
        return pl.ds(pl.multiple_of(i * rows, rows), rows)

    def block_rows(b):
        return pl.ds(pl.multiple_of(b * BLK, BLK), BLK)

    def own_copy(i):
        return pltpu.make_async_copy(feats.at[group_rows(i)], own.at[group_rows(i)], own_sem.at[i])

    def w_copy(j):
        source = w_qkv.at[:, pl.ds(j * rows, rows)] if j < 6 else w_out.at[:, pl.ds((j - 6) * rows, rows)]
        return pltpu.make_async_copy(source, summed.at[j], w_sem.at[j])

    def out_copy(i):
        return pltpu.make_async_copy(own.at[group_rows(i)], out.at[group_rows(i)], out_sem.at[i])

    def remote(source, target, send, recv, device):
        return pltpu.make_async_remote_copy(
            src_ref=source, dst_ref=target, send_sem=send, recv_sem=recv,
            device_id=device, device_id_type=MESH,
        )

    def x_copy(c):
        return remote(feats.at[block_rows(c)], near.at[block_rows(c)], x_send.at[c], x_recv.at[c], (mate, seg))

    def z_copy(c):
        return remote(near.at[block_rows(c)], far.at[block_rows(c)], z_send.at[c], z_recv.at[c], (ahead, seg))

    def h_copy(j):
        b, device = ((blocks - 1), (line, right)) if j == 0 else (0, (line, left))
        return remote(feats.at[pl.ds(b * BLK, BLK)], halo.at[pl.ds(j * BLK, BLK)], h_send.at[j], h_recv.at[j], device)

    def c_copy(j):
        source = cnt.at[2] if j == 3 else counts_row
        device = ((line, right), (line, left), (mate, seg), (ahead, seg))[j]
        return remote(source, cnt.at[j], c_send.at[j], c_recv.at[j], device)

    barrier = pltpu.get_barrier_semaphore()
    for device in ((mate, seg), (ahead, seg), (behind, seg), (line, right), (line, left)):
        pl.semaphore_signal(barrier, inc=1, device_id=device, device_id_type=MESH)
    for i in range(groups):
        own_copy(i).start()
    for j in range(8):
        w_copy(j).start()
    lane = iota((8, BLK), 1)
    filled = jnp.zeros((8, BLK), F32)
    for b in range(blocks):
        filled = jnp.where(lane == b, counts[0, b].astype(F32), filled)
    counts_row[...] = filled
    pl.semaphore_wait(barrier, 5)
    for j in range(3):
        c_copy(j).start()
    for j in range(2):
        h_copy(j).start()

    @pl.loop(0, blocks)
    def _(c):
        x_copy(c).start()

    for j in range(8):
        w_copy(j).wait()
        w = summed[j]
        if j < 2:
            w = w * (DIM**-0.5 * math.log2(math.e))
        if j // 2 in (0, 2):
            w = w.T
            where = (pl.ds(j % 2 * rows, rows), slice(None))
        else:
            where = (slice(None), pl.ds(j % 2 * rows, rows))
        high, rest = split(w)
        w_hi[(j // 2, *where)] = high
        w_lo[(j // 2, *where)] = rest

    def low(n):
        return iota((n, PAIR), 1) < DIM

    def mark(n):
        return iota((n, PAIR), 1) == DIM

    def weights(j, p):
        columns = pl.ds(p * rows, rows)
        return w_hi[j, :, columns], w_lo[j, :, columns]

    def project_across(j, xh, xl):
        wh, wl = w_hi[j], w_lo[j]
        return split(dot_nt(wh, xh) + dot_nt(wh, xl) + dot_nt(wl, xh))

    def bias_of(count):
        dead = (iota((BLK, PAIR), 0) >= count) & mark(BLK)
        return jnp.where(dead, MASKED, 0.0)

    def count_in(row, b):
        return jnp.sum(jnp.where(iota(row.shape, 1) == b, row, 0.0), axis=1, keepdims=True).astype(jnp.int32)

    def store_keys(xh, xl, k_ref, v_ref, slots, bias):
        lo = low(rows)
        for p in range(pairs // 2):
            both = dot3(xh, xl, *weights(1, p))
            for half in range(2):
                h = 4 * p + 2 * half
                k = both[:, half * PAIR : (half + 1) * PAIR]
                kh = k.astype(BF16).astype(F32)
                kl = k - kh
                kh_, kl_ = swap(kh), swap(kl)
                for head, a, b in ((h, jnp.where(lo, kh, kl_), kh), (h + 1, jnp.where(lo, kh_, kl), kh_)):
                    a = a.astype(BF16)
                    b = jnp.where(lo, b, bias).astype(BF16)
                    for n, slot in enumerate(slots):
                        k_ref[slot, head, :, :PAIR] = a[n * BLK : (n + 1) * BLK]
                        k_ref[slot, head, :, PAIR:] = b[n * BLK : (n + 1) * BLK]
        vh, vl = project_across(2, xh, xl)
        for h in range(HEADS):
            for n, slot in enumerate(slots):
                part = (slice(h * DIM, (h + 1) * DIM), slice(n * BLK, (n + 1) * BLK))
                v_ref[slot, h, :DIM] = vh[part]
                v_ref[slot, h, DIM:] = vl[part]

    def own_group(i):
        own_copy(i).wait()
        xh, xl = split(normalize(own[group_rows(i)], gain[...]))
        q_hi[i], q_lo[i] = project_across(0, xh, xl)
        bias = jnp.concatenate([bias_of(counts[0, 2 * i]), bias_of(counts[0, 2 * i + 1])], axis=0)
        slot = lax.rem(2 * i, RING)
        store_keys(xh, xl, k_ring, v_ring, (slot, slot + 1), bias)

    def halo_group():
        for j in range(2):
            h_copy(j).wait()
            c_copy(j).wait()
        xh, xl = split(normalize(halo[...], gain[...]))
        before = jnp.where(seg == 0, 0, count_in(cnt[0, 0:1], blocks - 1))
        after = jnp.where(seg == segs - 1, 0, count_in(cnt[1, 0:1], 0))
        bias = jnp.concatenate([bias_of(before), bias_of(after)], axis=0)
        store_keys(xh, xl, k_ring, v_ring, (RING - 1, RING), bias)

    use_near = lax.rem(partner[0, 0] + odd, 2) == 1

    def strip_group(i):
        z_copy(2 * i).wait_recv()
        z_copy(2 * i + 1).wait_recv()
        x = jnp.where(use_near, near[group_rows(i)], far[group_rows(i)])
        row = jnp.where(use_near, cnt[2, 0:1], cnt[3, 0:1])
        xh, xl = split(normalize(x, gain[...]))
        bias = jnp.concatenate([bias_of(count_in(row, 2 * i)), bias_of(count_in(row, 2 * i + 1))], axis=0)
        store_keys(xh, xl, k_strip, v_strip, (2 * i, 2 * i + 1), bias)

    def queries(i, h):
        part = slice(h * DIM, (h + 1) * DIM)
        one = jnp.where(iota((DIM, rows), 0) == 0, 1.0, 0.0).astype(BF16)
        return jnp.concatenate([q_hi[i, part], q_hi[i, part], q_lo[i, part], one], axis=0)

    def weigh(s, top, v):
        e = jnp.exp2(s - top)
        both = dot(v, jnp.concatenate(split(e), axis=1))
        both = both[:, :BLK] + both[:, BLK:]
        return both[:DIM] + both[DIM:], jnp.sum(e, axis=0, keepdims=True)

    def local_group(i, last=False):
        slots = [lax.rem(2 * i - 1 + j + RING, RING) for j in range(4)]
        if last:
            slots[3] = RING
        for h in range(HEADS):
            k = jnp.concatenate([k_ring[slot, h] for slot in slots], axis=0)
            v = jnp.concatenate([v_ring[slot, h] for slot in slots], axis=1)
            scores = dot(k, queries(i, h))
            for n in range(2):
                columns = slice(n * BLK, (n + 1) * BLK)
                keys = slice(n * BLK, (n + 3) * BLK)
                s = scores[keys, columns]
                top = jnp.max(s, axis=0, keepdims=True)
                part, total = weigh(s, top, v[:, keys])
                summed[i, h * DIM : (h + 1) * DIM, columns] = part
                tops[i, h : h + 1, columns] = top
                totals[i, h : h + 1, columns] = total

    for h in range(HEADS):
        k_strip[blocks, h, :, :PAIR] = jnp.zeros((BLK, PAIR), BF16)
        k_strip[blocks, h, :, PAIR:] = bias_of(0).astype(BF16)
        v_strip[blocks, h] = jnp.zeros((BLK, PAIR), BF16)

    @pl.loop(0, groups)
    def _(i):
        x_copy(2 * i).wait_recv()
        z_copy(2 * i).start()

        @pl.when(i == 0)
        def _():
            c_copy(2).wait()
            c_copy(3).start()

        own_group(i)
        x_copy(2 * i + 1).wait_recv()
        z_copy(2 * i + 1).start()

        @pl.when(i == 0)
        def _():
            halo_group()
            c_copy(3).wait()

        @pl.when(i > 0)
        def _():
            local_group(i - 1)
            strip_group(i - 1)

    local_group(groups - 1, last=True)
    strip_group(groups - 1)

    @pl.loop(0, groups)
    def _(i):
        picks = [[jnp.where(listed[2 * i + n, j] < 0, blocks, listed[2 * i + n, j]) for j in range(2)] for n in range(2)]
        heads = []
        for h in range(HEADS):
            q = queries(i, h)
            parts = []
            for n in range(2):
                columns = slice(n * BLK, (n + 1) * BLK)
                k = jnp.concatenate([k_strip[pick, h] for pick in picks[n]], axis=0)
                v = jnp.concatenate([v_strip[pick, h] for pick in picks[n]], axis=1)
                s = dot(k, q[:, columns])
                before = tops[i, h : h + 1, columns]
                top = jnp.maximum(jnp.max(s, axis=0, keepdims=True), before)
                part, total = weigh(s, top, v)
                weight = jnp.exp2(before - top)
                total = total + totals[i, h : h + 1, columns] * weight
                part = part + summed[i, h * DIM : (h + 1) * DIM, columns] * weight
                parts.append(part * (1.0 / total))
            heads.append(jnp.concatenate(parts, axis=1))
        ah, al = split(jnp.concatenate(heads, axis=0).T)
        r = group_rows(i)
        row = iota((BLK, 2 * PAIR), 0)
        live = jnp.concatenate([row < counts[0, 2 * i + n] for n in range(2)], axis=0)
        for p in range(pairs // 2):
            columns = slice(p * 2 * PAIR, (p + 1) * 2 * PAIR)
            result = own[r, columns] + dot3(ah, al, *weights(3, p))
            own[r, columns] = jnp.where(live, result, 0.0)
        out_copy(i).start()

    @pl.loop(0, blocks)
    def _(c):
        x_copy(c).wait_send()
        z_copy(c).wait_send()

    for i in range(groups):
        out_copy(i).wait()


def body(feats, norm_gain, w_qkv, w_out, counts, partner, cross_list):
    points = feats[0]
    rows, width = points.shape
    blocks = counts.shape[1]
    groups = blocks // 2
    hbm = pl.BlockSpec(memory_space=pl.ANY)
    vmem = pl.BlockSpec(memory_space=pltpu.VMEM)
    smem = pl.BlockSpec(memory_space=pltpu.SMEM)
    dma = pltpu.SemaphoreType.DMA
    mixed = pl.pallas_call(
        functools.partial(kernel, blocks),
        out_shape=jax.ShapeDtypeStruct((rows, width), F32),
        in_specs=[hbm, vmem, hbm, hbm, smem, smem, smem],
        out_specs=hbm,
        scratch_shapes=[
            pltpu.VMEM((rows, width), F32),
            pltpu.VMEM((rows, width), F32),
            pltpu.VMEM((rows, width), F32),
            pltpu.VMEM((2 * BLK, width), F32),
            pltpu.VMEM((8, BLK), F32),
            pltpu.VMEM((4, 8, BLK), F32),
            pltpu.VMEM((4, width, width), BF16),
            pltpu.VMEM((4, width, width), BF16),
            pltpu.VMEM((groups, width, 2 * BLK), BF16),
            pltpu.VMEM((groups, width, 2 * BLK), BF16),
            pltpu.VMEM((RING + 1, HEADS, BLK, 2 * PAIR), BF16),
            pltpu.VMEM((RING + 1, HEADS, PAIR, BLK), BF16),
            pltpu.VMEM((blocks + 1, HEADS, BLK, 2 * PAIR), BF16),
            pltpu.VMEM((blocks + 1, HEADS, PAIR, BLK), BF16),
            pltpu.VMEM((groups, width, 2 * BLK), F32),
            pltpu.VMEM((groups, HEADS, 2 * BLK), F32),
            pltpu.VMEM((groups, HEADS, 2 * BLK), F32),
            dma((blocks,)), dma((blocks,)), dma((blocks,)), dma((blocks,)),
            dma((2,)), dma((2,)), dma((4,)), dma((4,)),
            dma((groups,)), dma((8,)), dma((groups,)),
        ],
        compiler_params=pltpu.CompilerParams(
            collective_id=0, has_side_effects=True, vmem_limit_bytes=60 * 1024 * 1024
        ),
    )(points, norm_gain.reshape(1, width), w_qkv, w_out, counts, partner, cross_list[0])
    return mixed[None]


def solution(mesh):
    in_specs = (
        P("line", "seg", None),
        P(),
        P(),
        P(),
        P("line", "seg"),
        P("line", "seg"),
        P("line", "seg", None),
    )
    out_specs = P("line", "seg", None)
    return jax.shard_map(body, mesh=mesh, in_specs=in_specs, out_specs=out_specs, check_vma=False)
```

time: 186 us -> 164 us (0.88)
  Pallas kernels: 177 us -> 158 us
  local copies, waits for them, and re-layouts: 8.12 us -> 5.99 us
    pallas_call x1, Pallas kernels: 177 us -> 158 us  [body(): pl.pallas_call(functools.partial(kernel, blocks), out_shape=jax.ShapeDtyp...]
where the time goes in v2:
time: 164 us
  Pallas kernels  158 us (96%)
  local copies, waits for them, and re-layouts  5.99 us (4%)
    pallas_call x1, Pallas kernels, body(): pl.pallas_call(functools.partial(kernel, blocks), out_shape=jax.ShapeDtyp...  158 us
    unnamed x1, local copies, waits for them, and re-layouts  4.64 us

profile of v2, /device:TPU:8, one launch (start us, length us, event | category | flops | bytes accessed | tf_op | source)
XLA Modules:
  0.0 164.3 jit_solution(7022988394090659413)
XLA Ops:
  0.7 1.4 copy.8.listed
  2.0 157.6 %shard_map.73 = f32[2048,512]{1,0:T(8,128)} custom-call(f32[2048,512]{1,0:T(8,128)} %bitcast.5, f32[1,512]{1,0:T(1,128)} %bitcast.6, f32[512,1536]{1,0:T(8,128)} %w_qkv.1, f32[512,512]{1,0:T(8,128)} %w_out.1, s32[1,16]{1,0:T(1,128)} %counts.1, s32[1,1]{1,0:T(1,128)S(6)} %copy.10.partner, s32[16,2]{1,0:T(8,128)} %copy.8.listed), custom_call_target="tpu_custom_call" | custom-call | tf_op jit(solution)/shard_map/pallas_call | solution.py:329
  159.7 4.6 %copy.11 = f32[1,2048,512]{2,1,0:T(8,128)} copy(f32[1,2048,512]{2,1,0:T(8,128)} %bitcast.4) | data formatting | bytes 8388608

commit v3 on v2

--- a/solution.py
+++ b/solution.py
@@ -15,6 +15,8 @@
 DIM = 64
 PAIR = 2 * DIM
 RING = 8
+BATCH = 4
+PIPED = True
 MASKED = -1e30
 NT = (((1,), (1,)), ((), ()))
 
@@ -222,29 +224,52 @@
         one = jnp.where(iota((DIM, rows), 0) == 0, 1.0, 0.0).astype(BF16)
         return jnp.concatenate([q_hi[i, part], q_hi[i, part], q_lo[i, part], one], axis=0)
 
-    def weigh(s, top, v):
-        e = jnp.exp2(s - top)
-        both = dot(v, jnp.concatenate(split(e), axis=1))
-        both = both[:, :BLK] + both[:, BLK:]
-        return both[:DIM] + both[DIM:], jnp.sum(e, axis=0, keepdims=True)
+    def tiled(x):
+        return x.reshape(-1, 8, BLK)
+
+    def over_rows(reduce, x):
+        return jnp.broadcast_to(reduce(reduce(tiled(x), axis=0), axis=0, keepdims=True), (8, BLK))
+
+    halves = [slice(n * BLK, (n + 1) * BLK) for n in range(2)]
+
+    def attend(score, values, floor, finish):
+        batches = [range(h, h + BATCH) for h in range(0, HEADS, BATCH)]
+        scores = [score(h) for h in batches[0]]
+        for number, batch in enumerate(batches):
+            items = [(h, n) for h in batch for n in range(2)]
+            flat = [s for pair in scores for s in pair]
+            if PIPED and number + 1 < len(batches):
+                scores = [score(h) for h in batches[number + 1]]
+            peaks = [over_rows(jnp.max, s) for s in flat]
+            peaks = [floor(h, n, top) for (h, n), top in zip(items, peaks)]
+            powers = [jnp.exp2(tiled(s) - top).reshape(s.shape) for s, top in zip(flat, peaks)]
+            sums = [over_rows(jnp.sum, e) for e in powers]
+            products = [dot(values(h, n), jnp.concatenate(split(e), axis=1)) for (h, n), e in zip(items, powers)]
+            if not PIPED and number + 1 < len(batches):
+                scores = [score(h) for h in batches[number + 1]]
+            for (h, n), both, total, top in zip(items, products, sums, peaks):
+                both = both[:, :BLK] + both[:, BLK:]
+                finish(h, n, both[:DIM] + both[DIM:], total, top)
 
     def local_group(i, last=False):
         slots = [lax.rem(2 * i - 1 + j + RING, RING) for j in range(4)]
         if last:
             slots[3] = RING
-        for h in range(HEADS):
+
+        def score(h):
             k = jnp.concatenate([k_ring[slot, h] for slot in slots], axis=0)
-            v = jnp.concatenate([v_ring[slot, h] for slot in slots], axis=1)
-            scores = dot(k, queries(i, h))
-            for n in range(2):
-                columns = slice(n * BLK, (n + 1) * BLK)
-                keys = slice(n * BLK, (n + 3) * BLK)
-                s = scores[keys, columns]
-                top = jnp.max(s, axis=0, keepdims=True)
-                part, total = weigh(s, top, v[:, keys])
-                summed[i, h * DIM : (h + 1) * DIM, columns] = part
-                tops[i, h : h + 1, columns] = top
-                totals[i, h : h + 1, columns] = total
+            s = dot(k, queries(i, h))
+            return [s[n * BLK : (n + 3) * BLK, halves[n]] for n in range(2)]
+
+        def values(h, n):
+            return jnp.concatenate([v_ring[slot, h] for slot in slots[n : n + 3]], axis=1)
+
+        def finish(h, n, part, total, top):
+            summed[i, h * DIM : (h + 1) * DIM, halves[n]] = part
+            tops[i, h, :, halves[n]] = top
+            totals[i, h, :, halves[n]] = total
+
+        attend(score, values, lambda h, n, top: top, finish)
 
     for h in range(HEADS):
         k_strip[blocks, h, :, :PAIR] = jnp.zeros((BLK, PAIR), BF16)
@@ -281,23 +306,26 @@
     @pl.loop(0, groups)
     def _(i):
         picks = [[jnp.where(listed[2 * i + n, j] < 0, blocks, listed[2 * i + n, j]) for j in range(2)] for n in range(2)]
-        heads = []
-        for h in range(HEADS):
+        heads = {}
+
+        def score(h):
             q = queries(i, h)
-            parts = []
-            for n in range(2):
-                columns = slice(n * BLK, (n + 1) * BLK)
-                k = jnp.concatenate([k_strip[pick, h] for pick in picks[n]], axis=0)
-                v = jnp.concatenate([v_strip[pick, h] for pick in picks[n]], axis=1)
-                s = dot(k, q[:, columns])
-                before = tops[i, h : h + 1, columns]
-                top = jnp.maximum(jnp.max(s, axis=0, keepdims=True), before)
-                part, total = weigh(s, top, v)
-                weight = jnp.exp2(before - top)
-                total = total + totals[i, h : h + 1, columns] * weight
-                part = part + summed[i, h * DIM : (h + 1) * DIM, columns] * weight
-                parts.append(part * (1.0 / total))
-            heads.append(jnp.concatenate(parts, axis=1))
+            return [dot(jnp.concatenate([k_strip[pick, h] for pick in picks[n]], axis=0), q[:, halves[n]]) for n in range(2)]
+
+        def values(h, n):
+            return jnp.concatenate([v_strip[pick, h] for pick in picks[n]], axis=1)
+
+        def floor(h, n, top):
+            return jnp.maximum(top, tops[i, h, :, halves[n]])
+
+        def finish(h, n, part, total, top):
+            weight = jnp.exp2(tops[i, h, :, halves[n]] - top)
+            total = total + totals[i, h, :, halves[n]] * weight
+            part = tiled(part) + tiled(summed[i, h * DIM : (h + 1) * DIM, halves[n]]) * weight
+            heads[h, n] = (part * (1.0 / total)).reshape(DIM, BLK)
+
+        attend(score, values, floor, finish)
+        heads = [jnp.concatenate([heads[h, 0], heads[h, 1]], axis=1) for h in range(HEADS)]
         ah, al = split(jnp.concatenate(heads, axis=0).T)
         r = group_rows(i)
         row = iota((BLK, 2 * PAIR), 0)
@@ -347,8 +375,8 @@
             pltpu.VMEM((blocks + 1, HEADS, BLK, 2 * PAIR), BF16),
             pltpu.VMEM((blocks + 1, HEADS, PAIR, BLK), BF16),
             pltpu.VMEM((groups, width, 2 * BLK), F32),
-            pltpu.VMEM((groups, HEADS, 2 * BLK), F32),
-            pltpu.VMEM((groups, HEADS, 2 * BLK), F32),
+            pltpu.VMEM((groups, HEADS, 8, 2 * BLK), F32),
+            pltpu.VMEM((groups, HEADS, 8, 2 * BLK), F32),
             dma((blocks,)), dma((blocks,)), dma((blocks,)), dma((blocks,)),
             dma((2,)), dma((2,)), dma((4,)), dma((4,)),
             dma((groups,)), dma((8,)), dma((groups,)),

time: 164 us -> 138 us (0.84)
  Pallas kernels: 158 us -> 131 us
    pallas_call x1, Pallas kernels: 158 us -> 131 us  [body(): pl.pallas_call(functools.partial(kernel, blocks), out_shape=jax.ShapeDtyp...]
where the time goes in v3:
time: 138 us
  Pallas kernels  131 us (95%)
  local copies, waits for them, and re-layouts  5.99 us (4%)
    pallas_call x1, Pallas kernels, body(): pl.pallas_call(functools.partial(kernel, blocks), out_shape=jax.ShapeDtyp...  131 us
    unnamed x1, local copies, waits for them, and re-layouts  4.64 us

profile of v3, /device:TPU:8, one launch (start us, length us, event | category | flops | bytes accessed | tf_op | source)
XLA Modules:
  0.0 137.9 jit_solution(12394979015189934941)
XLA Ops:
  0.7 1.4 copy.8.listed
  2.0 131.2 %shard_map.73 = f32[2048,512]{1,0:T(8,128)} custom-call(f32[2048,512]{1,0:T(8,128)} %bitcast.5, f32[1,512]{1,0:T(1,128)} %bitcast.6, f32[512,1536]{1,0:T(8,128)} %w_qkv.1, f32[512,512]{1,0:T(8,128)} %w_out.1, s32[1,16]{1,0:T(1,128)} %counts.1, s32[1,1]{1,0:T(1,128)S(6)} %copy.10.partner, s32[16,2]{1,0:T(8,128)} %copy.8.listed), custom_call_target="tpu_custom_call" | custom-call | tf_op jit(solution)/shard_map/pallas_call | solution.py:357
  133.2 4.6 %copy.11 = f32[1,2048,512]{2,1,0:T(8,128)} copy(f32[1,2048,512]{2,1,0:T(8,128)} %bitcast.4) | data formatting | bytes 8388608

commit v4 on v3

--- a/solution.py
+++ b/solution.py
@@ -14,7 +14,7 @@
 BLK = 128
 DIM = 64
 PAIR = 2 * DIM
-RING = 8
+CHUNK = 64
 BATCH = 4
 PIPED = True
 MASKED = -1e30
@@ -57,12 +57,13 @@
     feats, gain, w_qkv, w_out, counts, partner, listed,
     out,
     own, near, far, halo, counts_row, cnt,
-    w_hi, w_lo, q_hi, q_lo, k_ring, v_ring, k_strip, v_strip, summed, tops, totals,
+    w_hi, w_lo, q_hi, q_lo, k_own, v_own, k_strip, v_strip, summed, tops, totals,
     x_send, x_recv, z_send, z_recv, h_send, h_recv, c_send, c_recv,
     own_sem, w_sem, out_sem,
 ):
     groups = blocks // 2
     rows = 2 * BLK
+    each = rows // CHUNK
     width = own.shape[1]
     pairs = width // PAIR
     line, seg = lax.axis_index("line"), lax.axis_index("seg")
@@ -76,8 +77,8 @@
     def group_rows(i):
         return pl.ds(pl.multiple_of(i * rows, rows), rows)
 
-    def block_rows(b):
-        return pl.ds(pl.multiple_of(b * BLK, BLK), BLK)
+    def chunk_rows(c):
+        return pl.ds(pl.multiple_of(c * CHUNK, CHUNK), CHUNK)
 
     def own_copy(i):
         return pltpu.make_async_copy(feats.at[group_rows(i)], own.at[group_rows(i)], own_sem.at[i])
@@ -96,10 +97,10 @@
         )
 
     def x_copy(c):
-        return remote(feats.at[block_rows(c)], near.at[block_rows(c)], x_send.at[c], x_recv.at[c], (mate, seg))
+        return remote(feats.at[chunk_rows(c)], near.at[chunk_rows(c)], x_send.at[c], x_recv.at[c], (mate, seg))
 
     def z_copy(c):
-        return remote(near.at[block_rows(c)], far.at[block_rows(c)], z_send.at[c], z_recv.at[c], (ahead, seg))
+        return remote(near.at[chunk_rows(c)], far.at[chunk_rows(c)], z_send.at[c], z_recv.at[c], (ahead, seg))
 
     def h_copy(j):
         b, device = ((blocks - 1), (line, right)) if j == 0 else (0, (line, left))
@@ -128,7 +129,7 @@
     for j in range(2):
         h_copy(j).start()
 
-    @pl.loop(0, blocks)
+    @pl.loop(0, groups * each)
     def _(c):
         x_copy(c).start()
 
@@ -195,8 +196,7 @@
         xh, xl = split(normalize(own[group_rows(i)], gain[...]))
         q_hi[i], q_lo[i] = project_across(0, xh, xl)
         bias = jnp.concatenate([bias_of(counts[0, 2 * i]), bias_of(counts[0, 2 * i + 1])], axis=0)
-        slot = lax.rem(2 * i, RING)
-        store_keys(xh, xl, k_ring, v_ring, (slot, slot + 1), bias)
+        store_keys(xh, xl, k_own, v_own, (2 * i, 2 * i + 1), bias)
 
     def halo_group():
         for j in range(2):
@@ -206,13 +206,13 @@
         before = jnp.where(seg == 0, 0, count_in(cnt[0, 0:1], blocks - 1))
         after = jnp.where(seg == segs - 1, 0, count_in(cnt[1, 0:1], 0))
         bias = jnp.concatenate([bias_of(before), bias_of(after)], axis=0)
-        store_keys(xh, xl, k_ring, v_ring, (RING - 1, RING), bias)
+        store_keys(xh, xl, k_own, v_own, (blocks - 1, blocks), bias)
 
     use_near = lax.rem(partner[0, 0] + odd, 2) == 1
 
     def strip_group(i):
-        z_copy(2 * i).wait_recv()
-        z_copy(2 * i + 1).wait_recv()
+        for n in range(each):
+            z_copy(each * i + n).wait_recv()
         x = jnp.where(use_near, near[group_rows(i)], far[group_rows(i)])
         row = jnp.where(use_near, cnt[2, 0:1], cnt[3, 0:1])
         xh, xl = split(normalize(x, gain[...]))
@@ -252,17 +252,17 @@
                 finish(h, n, both[:DIM] + both[DIM:], total, top)
 
     def local_group(i, last=False):
-        slots = [lax.rem(2 * i - 1 + j + RING, RING) for j in range(4)]
+        slots = [lax.rem(2 * i - 1 + j + blocks, blocks) for j in range(4)]
         if last:
-            slots[3] = RING
+            slots[3] = blocks
 
         def score(h):
-            k = jnp.concatenate([k_ring[slot, h] for slot in slots], axis=0)
+            k = jnp.concatenate([k_own[slot, h] for slot in slots], axis=0)
             s = dot(k, queries(i, h))
             return [s[n * BLK : (n + 3) * BLK, halves[n]] for n in range(2)]
 
         def values(h, n):
-            return jnp.concatenate([v_ring[slot, h] for slot in slots[n : n + 3]], axis=1)
+            return jnp.concatenate([v_own[slot, h] for slot in slots[n : n + 3]], axis=1)
 
         def finish(h, n, part, total, top):
             summed[i, h * DIM : (h + 1) * DIM, halves[n]] = part
@@ -276,36 +276,61 @@
         k_strip[blocks, h, :, PAIR:] = bias_of(0).astype(BF16)
         v_strip[blocks, h] = jnp.zeros((BLK, PAIR), BF16)
 
+    def pass_on(c):
+        x_copy(c).wait_recv()
+        z_copy(c).start()
+
+    half = groups // 2
+
+    @pl.loop(0, groups)
+    def _(j):
+        pass_on(each * j)
+
+        @pl.when(j == 0)
+        def _():
+            c_copy(2).wait()
+            c_copy(3).start()
+
+        @pl.when(j < half)
+        def _():
+            own_group(2 * j)
+
+        pass_on(each * j + 1)
+
+        @pl.when(j < half)
+        def _():
+            own_group(2 * j + 1)
+
+        @pl.when(j == 0)
+        def _():
+            halo_group()
+            c_copy(3).wait()
+
+        pass_on(each * j + 2)
+
+        @pl.when((j >= 1) & (j <= half))
+        def _():
+            local_group(2 * j - 2)
+
+        pass_on(each * j + 3)
+
+        @pl.when((j >= 1) & (j < half))
+        def _():
+            local_group(2 * j - 1)
+
+        @pl.when(j == half)
+        def _():
+            local_group(groups - 1, last=True)
+
+        @pl.when(j >= 1)
+        def _():
+            strip_group(j - 1)
+
+    strip_group(groups - 1)
+
     @pl.loop(0, groups)
     def _(i):
-        x_copy(2 * i).wait_recv()
-        z_copy(2 * i).start()
-
-        @pl.when(i == 0)
-        def _():
-            c_copy(2).wait()
-            c_copy(3).start()
-
-        own_group(i)
-        x_copy(2 * i + 1).wait_recv()
-        z_copy(2 * i + 1).start()
-
-        @pl.when(i == 0)
-        def _():
-            halo_group()
-            c_copy(3).wait()
-
-        @pl.when(i > 0)
-        def _():
-            local_group(i - 1)
-            strip_group(i - 1)
-
-    local_group(groups - 1, last=True)
-    strip_group(groups - 1)
-
-    @pl.loop(0, groups)
-    def _(i):
-        picks = [[jnp.where(listed[2 * i + n, j] < 0, blocks, listed[2 * i + n, j]) for j in range(2)] for n in range(2)]
+        picks = [[jnp.where(listed[j, 2 * i + n] < 0, blocks, listed[j, 2 * i + n]) for j in range(2)] for n in range(2)]
         heads = {}
 
         def score(h):
@@ -336,7 +361,7 @@
             own[r, columns] = jnp.where(live, result, 0.0)
         out_copy(i).start()
 
-    @pl.loop(0, blocks)
+    @pl.loop(0, groups * each)
     def _(c):
         x_copy(c).wait_send()
         z_copy(c).wait_send()
@@ -349,7 +374,7 @@
     points = feats[0]
     rows, width = points.shape
     blocks = counts.shape[1]
-    groups = blocks // 2
+    groups, chunks = blocks // 2, rows // CHUNK
     hbm = pl.BlockSpec(memory_space=pl.ANY)
     vmem = pl.BlockSpec(memory_space=pltpu.VMEM)
     smem = pl.BlockSpec(memory_space=pltpu.SMEM)
@@ -370,21 +395,21 @@
             pltpu.VMEM((4, width, width), BF16),
             pltpu.VMEM((groups, width, 2 * BLK), BF16),
             pltpu.VMEM((groups, width, 2 * BLK), BF16),
-            pltpu.VMEM((RING + 1, HEADS, BLK, 2 * PAIR), BF16),
-            pltpu.VMEM((RING + 1, HEADS, PAIR, BLK), BF16),
+            pltpu.VMEM((blocks + 1, HEADS, BLK, 2 * PAIR), BF16),
+            pltpu.VMEM((blocks + 1, HEADS, PAIR, BLK), BF16),
             pltpu.VMEM((blocks + 1, HEADS, BLK, 2 * PAIR), BF16),
             pltpu.VMEM((blocks + 1, HEADS, PAIR, BLK), BF16),
             pltpu.VMEM((groups, width, 2 * BLK), F32),
             pltpu.VMEM((groups, HEADS, 8, 2 * BLK), F32),
             pltpu.VMEM((groups, HEADS, 8, 2 * BLK), F32),
-            dma((blocks,)), dma((blocks,)), dma((blocks,)), dma((blocks,)),
+            dma((chunks,)), dma((chunks,)), dma((chunks,)), dma((chunks,)),
             dma((2,)), dma((2,)), dma((4,)), dma((4,)),
             dma((groups,)), dma((8,)), dma((groups,)),
         ],
         compiler_params=pltpu.CompilerParams(
             collective_id=0, has_side_effects=True, vmem_limit_bytes=60 * 1024 * 1024
         ),
-    )(points, norm_gain.reshape(1, width), w_qkv, w_out, counts, partner, cross_list[0])
+    )(points, norm_gain.reshape(1, width), w_qkv, w_out, counts, partner, cross_list[0].T)
     return mixed[None]
 
 

time: 138 us -> 134 us (0.971)
  Pallas kernels: 131 us -> 129 us
    pallas_call x1, Pallas kernels: 131 us -> 129 us  [body(): pl.pallas_call(functools.partial(kernel, blocks), out_shape=jax.ShapeDtyp...]
where the time goes in v4:
time: 134 us
  Pallas kernels  129 us (96%)
  local copies, waits for them, and re-layouts  4.64 us (3%)
    pallas_call x1, Pallas kernels, body(): pl.pallas_call(functools.partial(kernel, blocks), out_shape=jax.ShapeDtyp...  129 us
    unnamed x1, local copies, waits for them, and re-layouts  4.64 us

profile of v4, /device:TPU:8, one launch (start us, length us, event | category | flops | bytes accessed | tf_op | source)
XLA Modules:
  0.0 134.0 jit_solution(9707072626971250765)
XLA Ops:
  0.7 128.7 %shard_map.73 = f32[2048,512]{1,0:T(8,128)} custom-call(f32[2048,512]{1,0:T(8,128)} %bitcast.7, f32[1,512]{1,0:T(1,128)} %bitcast.8, f32[512,1536]{1,0:T(8,128)} %w_qkv.1, f32[512,512]{1,0:T(8,128)} %w_out.1, s32[1,16]{1,0:T(1,128)} %counts.1, s32[1,1]{1,0:T(1,128)S(6)} %copy.9.partner, s32[2,16]{1,0:T(2,128)} %bitcast.9), custom_call_target="tpu_custom_call" | custom-call | tf_op jit(solution)/shard_map/pallas_call | solution.py:382
  129.4 4.6 %copy.10 = f32[1,2048,512]{2,1,0:T(8,128)} copy(f32[1,2048,512]{2,1,0:T(8,128)} %bitcast.6) | data formatting | bytes 8388608

commit v5 on v4

--- a/solution.py
+++ b/solution.py
@@ -15,6 +15,7 @@
 DIM = 64
 PAIR = 2 * DIM
 CHUNK = 64
+LATE = 4
 BATCH = 4
 PIPED = True
 MASKED = -1e30
@@ -52,14 +53,48 @@
     return pltpu.roll(x, DIM, 1)
 
 
+def tiled(x):
+    return x.reshape(-1, 8, BLK)
+
+
+def over_rows(reduce, x):
+    return jnp.broadcast_to(reduce(reduce(tiled(x), axis=0), axis=0, keepdims=True), (8, BLK))
+
+
+def attend(score, values, floor, finish, parts):
+    size = 2 * BATCH // parts
+    batches = [range(h, h + size) for h in range(0, HEADS, size)]
+    scores = [score(h) for h in batches[0]]
+    for number, batch in enumerate(batches):
+        items = [(h, n) for h in batch for n in range(parts)]
+        flat = [s for pair in scores for s in pair]
+        if PIPED and number + 1 < len(batches):
+            scores = [score(h) for h in batches[number + 1]]
+        peaks = [over_rows(jnp.max, s) for s in flat]
+        peaks = [floor(h, n, top) for (h, n), top in zip(items, peaks)]
+        powers = [jnp.exp2(tiled(s) - top).reshape(s.shape) for s, top in zip(flat, peaks)]
+        sums = [over_rows(jnp.sum, e) for e in powers]
+        products = [dot(values(h, n), jnp.concatenate(split(e), axis=1)) for (h, n), e in zip(items, powers)]
+        if not PIPED and number + 1 < len(batches):
+            scores = [score(h) for h in batches[number + 1]]
+        for (h, n), both, total, top in zip(items, products, sums, peaks):
+            both = both[:, :BLK] + both[:, BLK:]
+            finish(h, n, both[:DIM] + both[DIM:], total, top)
+
+
+def queries_of(high, low):
+    one = jnp.where(iota(high.shape, 0) == 0, 1.0, 0.0).astype(BF16)
+    return jnp.concatenate([high, high, low, one], axis=0)
+
+
 def kernel(
     blocks,
     feats, gain, w_qkv, w_out, counts, partner, listed,
-    out,
+    summed_out, tops_out, totals_out, q_hi_out, q_lo_out, k_out, v_out, w_hi_out, w_lo_out,
     own, near, far, halo, counts_row, cnt,
     w_hi, w_lo, q_hi, q_lo, k_own, v_own, k_strip, v_strip, summed, tops, totals,
     x_send, x_recv, z_send, z_recv, h_send, h_recv, c_send, c_recv,
-    own_sem, w_sem, out_sem,
+    own_sem, w_sem, s_sem, q_sem, k_sem, p_sem,
 ):
     groups = blocks // 2
     rows = 2 * BLK
@@ -87,8 +122,21 @@
         source = w_qkv.at[:, pl.ds(j * rows, rows)] if j < 6 else w_out.at[:, pl.ds((j - 6) * rows, rows)]
         return pltpu.make_async_copy(source, summed.at[j], w_sem.at[j])
 
-    def out_copy(i):
-        return pltpu.make_async_copy(own.at[group_rows(i)], out.at[group_rows(i)], out_sem.at[i])
+    def sums_out(i):
+        pairs_ = ((summed, summed_out), (tops, tops_out), (totals, totals_out))
+        return [pltpu.make_async_copy(a.at[i], b.at[i], s_sem.at[n, i]) for n, (a, b) in enumerate(pairs_)]
+
+    def queries_out(i):
+        pairs_ = ((q_hi, q_hi_out), (q_lo, q_lo_out))
+        return [pltpu.make_async_copy(a.at[i], b.at[i], q_sem.at[n, i]) for n, (a, b) in enumerate(pairs_)]
+
+    def keys_out(n):
+        source = pl.ds(blocks - LATE + 2 * n, 2 + n)
+        target = pl.ds(2 * n, 2 + n)
+        return [pltpu.make_async_copy(a.at[source], b.at[target], k_sem.at[m, n]) for m, (a, b) in enumerate(((k_strip, k_out), (v_strip, v_out)))]
+
+    def projection_out():
+        return [pltpu.make_async_copy(a.at[3], b, p_sem.at[m]) for m, (a, b) in enumerate(((w_hi, w_hi_out), (w_lo, w_lo_out)))]
 
     def remote(source, target, send, recv, device):
         return pltpu.make_async_remote_copy(
@@ -195,6 +243,8 @@
         own_copy(i).wait()
         xh, xl = split(normalize(own[group_rows(i)], gain[...]))
         q_hi[i], q_lo[i] = project_across(0, xh, xl)
+        for copy in queries_out(i):
+            copy.start()
         bias = jnp.concatenate([bias_of(counts[0, 2 * i]), bias_of(counts[0, 2 * i + 1])], axis=0)
         store_keys(xh, xl, k_own, v_own, (2 * i, 2 * i + 1), bias)
 
@@ -221,35 +271,9 @@
 
     def queries(i, h):
         part = slice(h * DIM, (h + 1) * DIM)
-        one = jnp.where(iota((DIM, rows), 0) == 0, 1.0, 0.0).astype(BF16)
-        return jnp.concatenate([q_hi[i, part], q_hi[i, part], q_lo[i, part], one], axis=0)
-
-    def tiled(x):
-        return x.reshape(-1, 8, BLK)
-
-    def over_rows(reduce, x):
-        return jnp.broadcast_to(reduce(reduce(tiled(x), axis=0), axis=0, keepdims=True), (8, BLK))
+        return queries_of(q_hi[i, part], q_lo[i, part])
 
     halves = [slice(n * BLK, (n + 1) * BLK) for n in range(2)]
-
-    def attend(score, values, floor, finish):
-        batches = [range(h, h + BATCH) for h in range(0, HEADS, BATCH)]
-        scores = [score(h) for h in batches[0]]
-        for number, batch in enumerate(batches):
-            items = [(h, n) for h in batch for n in range(2)]
-            flat = [s for pair in scores for s in pair]
-            if PIPED and number + 1 < len(batches):
-                scores = [score(h) for h in batches[number + 1]]
-            peaks = [over_rows(jnp.max, s) for s in flat]
-            peaks = [floor(h, n, top) for (h, n), top in zip(items, peaks)]
-            powers = [jnp.exp2(tiled(s) - top).reshape(s.shape) for s, top in zip(flat, peaks)]
-            sums = [over_rows(jnp.sum, e) for e in powers]
-            products = [dot(values(h, n), jnp.concatenate(split(e), axis=1)) for (h, n), e in zip(items, powers)]
-            if not PIPED and number + 1 < len(batches):
-                scores = [score(h) for h in batches[number + 1]]
-            for (h, n), both, total, top in zip(items, products, sums, peaks):
-                both = both[:, :BLK] + both[:, BLK:]
-                finish(h, n, both[:DIM] + both[DIM:], total, top)
 
     def local_group(i, last=False):
         slots = [lax.rem(2 * i - 1 + j + blocks, blocks) for j in range(4)]
@@ -269,13 +293,47 @@
             tops[i, h, :, halves[n]] = top
             totals[i, h, :, halves[n]] = total
 
-        attend(score, values, lambda h, n, top: top, finish)
+        attend(score, values, lambda h, n, top: top, finish, 2)
 
     for h in range(HEADS):
         k_strip[blocks, h, :, :PAIR] = jnp.zeros((BLK, PAIR), BF16)
         k_strip[blocks, h, :, PAIR:] = bias_of(0).astype(BF16)
         v_strip[blocks, h] = jnp.zeros((BLK, PAIR), BF16)
 
+    for copy in projection_out():
+        copy.start()
+
+    def early_group(i):
+        def pick(j, b):
+            c = listed[j, b]
+            return jnp.where((c < 0) | (c >= blocks - LATE), blocks, c)
+
+        picks = [[pick(j, 2 * i + n) for j in range(2)] for n in range(2)]
+
+        def score(h):
+            q = queries(i, h)
+            return [dot(jnp.concatenate([k_strip[pick, h] for pick in picks[n]], axis=0), q[:, halves[n]]) for n in range(2)]
+
+        def values(h, n):
+            return jnp.concatenate([v_strip[pick, h] for pick in picks[n]], axis=1)
+
+        def floor(h, n, top):
+            return jnp.maximum(top, tops[i, h, :, halves[n]])
+
+        def finish(h, n, part, total, top):
+            weight = jnp.exp2(tops[i, h, :, halves[n]] - top)
+            here = slice(h * DIM, (h + 1) * DIM)
+            totals[i, h, :, halves[n]] = total + totals[i, h, :, halves[n]] * weight
+            summed[i, here, halves[n]] = (tiled(part) + tiled(summed[i, here, halves[n]]) * weight).reshape(DIM, BLK)
+            tops[i, h, :, halves[n]] = top
+
+        attend(score, values, floor, finish, 2)
+        for copy in sums_out(i):
+            copy.start()
+
+    def early_groups(first):
+        pl.loop(first, first + 2)(early_group)
+
     def pass_on(c):
         x_copy(c).wait_recv()
         z_copy(c).start()
@@ -295,6 +353,10 @@
         def _():
             own_group(2 * j)
 
+        @pl.when(j == groups - 1)
+        def _():
+            early_groups(2)
+
         pass_on(each * j + 1)
 
         @pl.when(j < half)
@@ -306,12 +368,20 @@
             halo_group()
             c_copy(3).wait()
 
+        @pl.when(j == groups - 1)
+        def _():
+            early_groups(4)
+
         pass_on(each * j + 2)
 
         @pl.when((j >= 1) & (j <= half))
         def _():
             local_group(2 * j - 2)
 
+        @pl.when(j == groups - 1)
+        def _():
+            early_groups(6)
+
         pass_on(each * j + 3)
 
         @pl.when((j >= 1) & (j < half))
@@ -326,48 +396,77 @@
         def _():
             strip_group(j - 1)
 
+        @pl.when(j == groups - 2)
+        def _():
+            early_groups(0)
+
+    for copy in keys_out(0):
+        copy.start()
     strip_group(groups - 1)
 
-    @pl.loop(0, groups)
-    def _(i):
-        picks = [[jnp.where(listed[j, 2 * i + n] < 0, blocks, listed[j, 2 * i + n]) for j in range(2)] for n in range(2)]
-        heads = {}
-
-        def score(h):
-            q = queries(i, h)
-            return [dot(jnp.concatenate([k_strip[pick, h] for pick in picks[n]], axis=0), q[:, halves[n]]) for n in range(2)]
-
-        def values(h, n):
-            return jnp.concatenate([v_strip[pick, h] for pick in picks[n]], axis=1)
-
-        def floor(h, n, top):
-            return jnp.maximum(top, tops[i, h, :, halves[n]])
-
-        def finish(h, n, part, total, top):
-            weight = jnp.exp2(tops[i, h, :, halves[n]] - top)
-            total = total + totals[i, h, :, halves[n]] * weight
-            part = tiled(part) + tiled(summed[i, h * DIM : (h + 1) * DIM, halves[n]]) * weight
-            heads[h, n] = (part * (1.0 / total)).reshape(DIM, BLK)
-
-        attend(score, values, floor, finish)
-        heads = [jnp.concatenate([heads[h, 0], heads[h, 1]], axis=1) for h in range(HEADS)]
-        ah, al = split(jnp.concatenate(heads, axis=0).T)
-        r = group_rows(i)
-        row = iota((BLK, 2 * PAIR), 0)
-        live = jnp.concatenate([row < counts[0, 2 * i + n] for n in range(2)], axis=0)
-        for p in range(pairs // 2):
-            columns = slice(p * 2 * PAIR, (p + 1) * 2 * PAIR)
-            result = own[r, columns] + dot3(ah, al, *weights(3, p))
-            own[r, columns] = jnp.where(live, result, 0.0)
-        out_copy(i).start()
+    for copy in keys_out(1):
+        copy.start()
 
     @pl.loop(0, groups * each)
     def _(c):
         x_copy(c).wait_send()
         z_copy(c).wait_send()
 
-    for i in range(groups):
-        out_copy(i).wait()
+    @pl.loop(0, groups)
+    def _(i):
+        for copy in sums_out(i) + queries_out(i):
+            copy.wait()
+
+    for copy in keys_out(0) + keys_out(1) + projection_out():
+        copy.wait()
+
+
+def finish_kernel(
+    blocks, counts, listed, summed, tops, totals, q_hi, q_lo, k_late, v_late, w_hi, w_lo, feats, out, sums, peaks, weights
+):
+    i = pl.program_id(0)
+    sums[...] = summed[0]
+    peaks[...] = tops[0]
+    weights[...] = totals[0]
+
+    @pl.loop(0, 4)
+    def _(t):
+        n, j = t // 2, lax.rem(t, 2)
+        pick = listed[j, 2 * i + n] - (blocks - LATE)
+
+        @pl.when(pick >= 0)
+        def _():
+            columns = pl.ds(pl.multiple_of(n * BLK, BLK), BLK)
+
+            def score(h):
+                here = slice(h * DIM, (h + 1) * DIM)
+                return [dot(k_late[pick, h], queries_of(q_hi[0, here, columns], q_lo[0, here, columns]))]
+
+            def floor(h, _, top):
+                return jnp.maximum(top, peaks[h, :, columns])
+
+            def finish(h, _, part, total, top):
+                weight = jnp.exp2(peaks[h, :, columns] - top)
+                here = slice(h * DIM, (h + 1) * DIM)
+                weights[h, :, columns] = total + weights[h, :, columns] * weight
+                sums[here, columns] = (tiled(part) + tiled(sums[here, columns]) * weight).reshape(DIM, BLK)
+                peaks[h, :, columns] = top
+
+            attend(score, lambda h, _: v_late[pick, h], floor, finish, 1)
+
+    rows = 2 * BLK
+    inverse = 1.0 / weights[...]
+    heads = []
+    for h in range(HEADS):
+        part = sums[h * DIM : (h + 1) * DIM].reshape(-1, 8, rows) * inverse[h]
+        heads.append(part.reshape(DIM, rows))
+    ah, al = split(jnp.concatenate(heads, axis=0).T)
+    row = iota((BLK, rows), 0)
+    live = jnp.concatenate([row < counts[0, 2 * i + n] for n in range(2)], axis=0)
+    for p in range(feats.shape[1] // rows):
+        columns = slice(p * rows, (p + 1) * rows)
+        result = feats[:, columns] + dot3(ah, al, w_hi[:, columns], w_lo[:, columns])
+        out[:, columns] = jnp.where(live, result, 0.0)
 
 
 def body(feats, norm_gain, w_qkv, w_out, counts, partner, cross_list):
@@ -379,11 +478,18 @@
     vmem = pl.BlockSpec(memory_space=pltpu.VMEM)
     smem = pl.BlockSpec(memory_space=pltpu.SMEM)
     dma = pltpu.SemaphoreType.DMA
-    mixed = pl.pallas_call(
+    wide = (groups, width, 2 * BLK)
+    rowed = (groups, HEADS, 8, 2 * BLK)
+    shapes = [
+        (wide, F32), (rowed, F32), (rowed, F32), (wide, BF16), (wide, BF16),
+        ((LATE + 1, HEADS, BLK, 2 * PAIR), BF16), ((LATE + 1, HEADS, PAIR, BLK), BF16),
+        ((width, width), BF16), ((width, width), BF16),
+    ]
+    middle = pl.pallas_call(
         functools.partial(kernel, blocks),
-        out_shape=jax.ShapeDtypeStruct((rows, width), F32),
+        out_shape=[jax.ShapeDtypeStruct(*shape) for shape in shapes],
         in_specs=[hbm, vmem, hbm, hbm, smem, smem, smem],
-        out_specs=hbm,
+        out_specs=[hbm] * len(shapes),
         scratch_shapes=[
             pltpu.VMEM((rows, width), F32),
             pltpu.VMEM((rows, width), F32),
@@ -404,12 +510,36 @@
             pltpu.VMEM((groups, HEADS, 8, 2 * BLK), F32),
             dma((chunks,)), dma((chunks,)), dma((chunks,)), dma((chunks,)),
             dma((2,)), dma((2,)), dma((4,)), dma((4,)),
-            dma((groups,)), dma((8,)), dma((groups,)),
+            dma((groups,)), dma((8,)), dma((3, groups)), dma((2, groups)), dma((2, 2)), dma((2,)),
         ],
         compiler_params=pltpu.CompilerParams(
             collective_id=0, has_side_effects=True, vmem_limit_bytes=60 * 1024 * 1024
         ),
     )(points, norm_gain.reshape(1, width), w_qkv, w_out, counts, partner, cross_list[0].T)
+
+    def step(*shape):
+        return pl.BlockSpec((1, *shape), lambda i: (i,) + (0,) * len(shape))
+
+    def whole(*shape):
+        return pl.BlockSpec(shape, lambda i: (0,) * len(shape))
+
+    part = pl.BlockSpec((2 * BLK, width), lambda i: (i, 0))
+    mixed = pl.pallas_call(
+        functools.partial(finish_kernel, blocks),
+        out_shape=jax.ShapeDtypeStruct((rows, width), F32),
+        grid=(groups,),
+        in_specs=[smem, smem]
+        + [step(*shape[1:]) for shape, _ in shapes[:5]]
+        + [whole(*shape) for shape, _ in shapes[5:]]
+        + [part],
+        out_specs=part,
+        scratch_shapes=[
+            pltpu.VMEM(wide[1:], F32),
+            pltpu.VMEM(rowed[1:], F32),
+            pltpu.VMEM(rowed[1:], F32),
+        ],
+        compiler_params=pltpu.CompilerParams(vmem_limit_bytes=48 * 1024 * 1024),
+    )(counts, cross_list[0].T, *middle, points)
     return mixed[None]
 
 

time: 134 us -> 140 us (1.045)
  local copies, waits for them, and re-layouts: 4.64 us -> 7.07 us
  Pallas kernels: 129 us -> 131 us
    pallas_call x1 -> x2, Pallas kernels: 129 us -> 131 us  [the longest x1 116 us: body(): pl.pallas_call(functools.partial(kernel, blocks), out_shape=[jax.ShapeDty...]
    unnamed x1 -> x16, local copies, waits for them, and re-layouts: 4.64 us -> 7.07 us
where the time goes in v5:
time: 140 us; the launch traced here: 139 us
  Pallas kernels  131 us (94%)
  local copies, waits for them, and re-layouts  7.07 us (5%)
    pallas_call x1, Pallas kernels, body(): pl.pallas_call(functools.partial(kernel, blocks), out_shape=[jax.ShapeDty...  116 us
    pallas_call x1, Pallas kernels, body(): pl.pallas_call(functools.partial(finish_kernel, blocks), out_shape=jax.Sh...  15 us
    unnamed x16, local copies, waits for them, and re-layouts  7.07 us

profile of v5, /device:TPU:8, one launch (start us, length us, event | category | flops | bytes accessed | tf_op | source)
XLA Modules:
  0.0 139.1 jit_solution(16234626803577521775)
XLA Ops:
  0.7 0.0 copy-start.6
  0.7 0.0 copy-start.7
  0.7 116.4 %shard_map.73 = (f32[8,512,256]{2,1,0:T(8,128)}, f32[8,8,8,256]{3,2,1,0:T(8,128)}, f32[8,8,8,256]{3,2,1,0:T(8,128)}, bf16[8,512,256]{2,1,0:T(8,128)(2,1)}, bf16[...) custom-call(f32[2048,512]{1,0:T(8,128)} %bitcast.8, ...), custom_call_target="tpu_custom_call" | custom-call | tf_op jit(solution)/shard_map/pallas_call | solution.py:488
  117.1 0.0 copy-done.6
  117.1 0.0 copy-done.7
  117.1 0.0 copy-start
  117.1 1.6 %copy-done = bf16[8,512,256]{2,1,0:T(8,128)(2,1)S(1)} copy-done((bf16[8,512,256]{2,1,0:T(8,128)(2,1)S(1)}, bf16[8,512,256]{2,1,0:T(8,128)(2,1)}, u32[]{:S(2)}) %copy-start) | copy-done | bytes 2097176
  118.7 0.0 copy-start.1
  118.7 1.3 copy-done.1
  120.0 0.0 copy-start.2
  120.0 1.0 copy-done.2
  121.0 0.0 copy-start.3
  121.1 1.0 copy-done.3
  122.1 0.0 copy-start.4
  122.1 1.0 copy-done.4
  123.1 0.0 copy-start.5
  123.1 1.0 copy-done.5
  124.2 15.0 %shard_map.74 = f32[2048,512]{1,0:T(8,128)} custom-call(s32[1,16]{1,0:T(1,128)S(1)} %copy-done.7, s32[2,16]{1,0:T(2,128)S(1)} %bitcast.7, f32[8,512,256]{2,1,0:T(8,128)} %get-tuple-element.14.summed, f32[8,8,8,256]{3,2,1,0:T(8,128)S(1)} %copy-done.2, f32[8,8,8,256]{3,2,1,0:T(8,128)S(1)} %copy-done.3, bf16[8,512,256]{2,1,0:T(8,128)(2,1)S(1)} %copy-done, ...), custom_call_target="tpu_custom_call" | custom-call | tf_op jit(solution)/shard_map/pallas_call | solution.py:527
Async XLA Ops:
  0.7 116.4 %copy-start.6 = (s32[1,16,2]{1,2,0:T(2,128)S(1)}, s32[1,16,2]{1,2,0:T(2,128)}, u32[]{:S(2)}) copy-start(s32[1,16,2]{1,2,0:T(2,128)} %param.13) | copy-start | bytes 388
  0.7 116.4 %copy-start.7 = (s32[1,16]{1,0:T(1,128)S(1)}, s32[1,16]{1,0:T(1,128)}, u32[]{:S(2)}) copy-start(s32[1,16]{1,0:T(1,128)} %counts.3) | copy-start | bytes 196
  117.1 1.6 %copy-start = (bf16[8,512,256]{2,1,0:T(8,128)(2,1)S(1)}, bf16[8,512,256]{2,1,0:T(8,128)(2,1)}, u32[]{:S(2)}) copy-start(bf16[8,512,256]{2,1,0:T(8,128)(2,1)} %get-tuple-element.17.q_hi) | copy-start | bytes 6291460
  118.7 1.3 copy-start.1
  120.0 1.0 copy-start.2
  121.0 1.0 copy-start.3
  122.1 1.0 copy-start.4
  123.1 1.0 copy-start.5

commit v6 on v5

--- a/solution.py
+++ b/solution.py
@@ -422,51 +422,83 @@
 
 
 def finish_kernel(
-    blocks, counts, listed, summed, tops, totals, q_hi, q_lo, k_late, v_late, w_hi, w_lo, feats, out, sums, peaks, weights
+    blocks, counts, listed, summed_in, tops_in, totals_in, q_hi_in, q_lo_in, k_in, v_in, w_hi_in, w_lo_in, feats, out,
+    summed, tops, totals, q_hi, q_lo, k_late, v_late, w_hi, w_lo, rest, g_sem, a_sem, out_sem,
 ):
-    i = pl.program_id(0)
-    sums[...] = summed[0]
-    peaks[...] = tops[0]
-    weights[...] = totals[0]
-
-    @pl.loop(0, 4)
-    def _(t):
-        n, j = t // 2, lax.rem(t, 2)
-        pick = listed[j, 2 * i + n] - (blocks - LATE)
-
-        @pl.when(pick >= 0)
-        def _():
-            columns = pl.ds(pl.multiple_of(n * BLK, BLK), BLK)
-
-            def score(h):
-                here = slice(h * DIM, (h + 1) * DIM)
-                return [dot(k_late[pick, h], queries_of(q_hi[0, here, columns], q_lo[0, here, columns]))]
-
-            def floor(h, _, top):
-                return jnp.maximum(top, peaks[h, :, columns])
-
-            def finish(h, _, part, total, top):
-                weight = jnp.exp2(peaks[h, :, columns] - top)
-                here = slice(h * DIM, (h + 1) * DIM)
-                weights[h, :, columns] = total + weights[h, :, columns] * weight
-                sums[here, columns] = (tiled(part) + tiled(sums[here, columns]) * weight).reshape(DIM, BLK)
-                peaks[h, :, columns] = top
-
-            attend(score, lambda h, _: v_late[pick, h], floor, finish, 1)
-
+    groups = blocks // 2
     rows = 2 * BLK
-    inverse = 1.0 / weights[...]
-    heads = []
-    for h in range(HEADS):
-        part = sums[h * DIM : (h + 1) * DIM].reshape(-1, 8, rows) * inverse[h]
-        heads.append(part.reshape(DIM, rows))
-    ah, al = split(jnp.concatenate(heads, axis=0).T)
-    row = iota((BLK, rows), 0)
-    live = jnp.concatenate([row < counts[0, 2 * i + n] for n in range(2)], axis=0)
-    for p in range(feats.shape[1] // rows):
-        columns = slice(p * rows, (p + 1) * rows)
-        result = feats[:, columns] + dot3(ah, al, w_hi[:, columns], w_lo[:, columns])
-        out[:, columns] = jnp.where(live, result, 0.0)
+
+    def group_rows(i):
+        return pl.ds(pl.multiple_of(i * rows, rows), rows)
+
+    def group_copies(i):
+        refs = ((summed_in.at[i], summed.at[i]), (q_hi_in.at[i], q_hi.at[i]), (q_lo_in.at[i], q_lo.at[i]), (feats.at[group_rows(i)], rest.at[group_rows(i)]))
+        return [pltpu.make_async_copy(*pair, g_sem.at[n, i]) for n, pair in enumerate(refs)]
+
+    refs = ((k_in, k_late), (v_in, v_late), (tops_in, tops), (totals_in, totals), (w_hi_in, w_hi), (w_lo_in, w_lo))
+    shared = [pltpu.make_async_copy(*pair, a_sem.at[n]) for n, pair in enumerate(refs)]
+
+    def out_copy(i):
+        return pltpu.make_async_copy(rest.at[group_rows(i)], out.at[group_rows(i)], out_sem.at[i])
+
+    for copy in shared:
+        copy.start()
+
+    @pl.loop(0, groups)
+    def _(i):
+        for copy in group_copies(i):
+            copy.start()
+
+    for copy in shared:
+        copy.wait()
+
+    @pl.loop(0, groups)
+    def _(i):
+        for copy in group_copies(i):
+            copy.wait()
+
+        @pl.loop(0, 4)
+        def _(t):
+            n, j = t // 2, lax.rem(t, 2)
+            pick = listed[j, 2 * i + n] - (blocks - LATE)
+
+            @pl.when(pick >= 0)
+            def _():
+                columns = pl.ds(pl.multiple_of(n * BLK, BLK), BLK)
+
+                def score(h):
+                    here = slice(h * DIM, (h + 1) * DIM)
+                    return [dot(k_late[pick, h], queries_of(q_hi[i, here, columns], q_lo[i, here, columns]))]
+
+                def floor(h, _, top):
+                    return jnp.maximum(top, tops[i, h, :, columns])
+
+                def finish(h, _, part, total, top):
+                    weight = jnp.exp2(tops[i, h, :, columns] - top)
+                    here = slice(h * DIM, (h + 1) * DIM)
+                    totals[i, h, :, columns] = total + totals[i, h, :, columns] * weight
+                    summed[i, here, columns] = (tiled(part) + tiled(summed[i, here, columns]) * weight).reshape(DIM, BLK)
+                    tops[i, h, :, columns] = top
+
+                attend(score, lambda h, _: v_late[pick, h], floor, finish, 1)
+
+        inverse = 1.0 / totals[i]
+        heads = []
+        for h in range(HEADS):
+            part = summed[i, h * DIM : (h + 1) * DIM].reshape(-1, 8, rows) * inverse[h]
+            heads.append(part.reshape(DIM, rows))
+        ah, al = split(jnp.concatenate(heads, axis=0).T)
+        row = iota((BLK, rows), 0)
+        live = jnp.concatenate([row < counts[0, 2 * i + n] for n in range(2)], axis=0)
+        r = group_rows(i)
+        for p in range(rest.shape[1] // rows):
+            columns = slice(p * rows, (p + 1) * rows)
+            result = rest[r, columns] + dot3(ah, al, w_hi[:, columns], w_lo[:, columns])
+            rest[r, columns] = jnp.where(live, result, 0.0)
+        out_copy(i).start()
+
+    for i in range(groups):
+        out_copy(i).wait()
 
 
 def body(feats, norm_gain, w_qkv, w_out, counts, partner, cross_list):
@@ -517,28 +549,14 @@
         ),
     )(points, norm_gain.reshape(1, width), w_qkv, w_out, counts, partner, cross_list[0].T)
 
-    def step(*shape):
-        return pl.BlockSpec((1, *shape), lambda i: (i,) + (0,) * len(shape))
-
-    def whole(*shape):
-        return pl.BlockSpec(shape, lambda i: (0,) * len(shape))
-
-    part = pl.BlockSpec((2 * BLK, width), lambda i: (i, 0))
     mixed = pl.pallas_call(
         functools.partial(finish_kernel, blocks),
         out_shape=jax.ShapeDtypeStruct((rows, width), F32),
-        grid=(groups,),
-        in_specs=[smem, smem]
-        + [step(*shape[1:]) for shape, _ in shapes[:5]]
-        + [whole(*shape) for shape, _ in shapes[5:]]
-        + [part],
-        out_specs=part,
-        scratch_shapes=[
-            pltpu.VMEM(wide[1:], F32),
-            pltpu.VMEM(rowed[1:], F32),
-            pltpu.VMEM(rowed[1:], F32),
-        ],
-        compiler_params=pltpu.CompilerParams(vmem_limit_bytes=48 * 1024 * 1024),
+        in_specs=[smem, smem] + [hbm] * (len(shapes) + 1),
+        out_specs=hbm,
+        scratch_shapes=[pltpu.VMEM(*shape) for shape in shapes]
+        + [pltpu.VMEM((rows, width), F32), dma((4, groups)), dma((6,)), dma((groups,))],
+        compiler_params=pltpu.CompilerParams(vmem_limit_bytes=60 * 1024 * 1024),
     )(counts, cross_list[0].T, *middle, points)
     return mixed[None]
 

time: 140 us -> 133 us (0.950)
  local copies, waits for them, and re-layouts: 7.07 us -> 0 us
    unnamed x16 -> x0, local copies, waits for them, and re-layouts: 7.07 us -> none
where the time goes in v6:
time: 133 us
  Pallas kernels  132 us (99%)
    pallas_call x1, Pallas kernels, body(): pl.pallas_call(functools.partial(kernel, blocks), out_shape=[jax.ShapeDty...  116 us
    pallas_call x1, Pallas kernels, body(): pl.pallas_call(functools.partial(finish_kernel, blocks), out_shape=jax.Sh...  16.1 us

profile of v6, /device:TPU:8, one launch (start us, length us, event | category | flops | bytes accessed | tf_op | source)
XLA Modules:
  0.0 133.3 jit_solution(14096041800634615879)
XLA Ops:
  0.7 116.4 %shard_map.73 = (f32[8,512,256]{2,1,0:T(8,128)}, f32[8,8,8,256]{3,2,1,0:T(8,128)}, f32[8,8,8,256]{3,2,1,0:T(8,128)}, bf16[8,512,256]{2,1,0:T(8,128)(2,1)}, bf16[...) custom-call(f32[2048,512]{1,0:T(8,128)} %bitcast.6, ...), custom_call_target="tpu_custom_call" | custom-call | tf_op jit(solution)/shard_map/pallas_call | solution.py:520
  117.0 16.1 %shard_map.74 = f32[2048,512]{1,0:T(8,128)} custom-call(s32[1,16]{1,0:T(1,128)} %counts.3, s32[2,16]{1,0:T(2,128)} %bitcast.9, f32[8,512,256]{2,1,0:T(8,128)} %get-tuple-element.14.summed_in, f32[8,8,8,256]{3,2,1,0:T(8,128)} %get-tuple-element.15.tops_in, f32[8,8,8,256]{3,2,1,0:T(8,128)} %get-tuple-element.16.totals_in, ...), custom_call_target="tpu_custom_call" | custom-call | tf_op jit(solution)/shard_map/pallas_call | solution.py:552

commit v7 on v6

--- a/solution.py
+++ b/solution.py
@@ -90,7 +90,7 @@
 def kernel(
     blocks,
     feats, gain, w_qkv, w_out, counts, partner, listed,
-    summed_out, tops_out, totals_out, q_hi_out, q_lo_out, k_out, v_out, w_hi_out, w_lo_out,
+    summed_out, tops_out, totals_out, q_hi_out, q_lo_out, k_out, m_out, v_out, w_hi_out, w_lo_out,
     own, near, far, halo, counts_row, cnt,
     w_hi, w_lo, q_hi, q_lo, k_own, v_own, k_strip, v_strip, summed, tops, totals,
     x_send, x_recv, z_send, z_recv, h_send, h_recv, c_send, c_recv,
@@ -133,7 +133,12 @@
     def keys_out(n):
         source = pl.ds(blocks - LATE + 2 * n, 2 + n)
         target = pl.ds(2 * n, 2 + n)
-        return [pltpu.make_async_copy(a.at[source], b.at[target], k_sem.at[m, n]) for m, (a, b) in enumerate(((k_strip, k_out), (v_strip, v_out)))]
+        pairs_ = (
+            (k_strip.at[source, :, :, pl.ds(0, PAIR)], k_out),
+            (k_strip.at[source, 0, :, pl.ds(PAIR, PAIR)], m_out),
+            (v_strip.at[source], v_out),
+        )
+        return [pltpu.make_async_copy(a, b.at[target], k_sem.at[m, n]) for m, (a, b) in enumerate(pairs_)]
 
     def projection_out():
         return [pltpu.make_async_copy(a.at[3], b, p_sem.at[m]) for m, (a, b) in enumerate(((w_hi, w_hi_out), (w_lo, w_lo_out)))]
@@ -422,8 +427,8 @@
 
 
 def finish_kernel(
-    blocks, counts, listed, summed_in, tops_in, totals_in, q_hi_in, q_lo_in, k_in, v_in, w_hi_in, w_lo_in, feats, out,
-    summed, tops, totals, q_hi, q_lo, k_late, v_late, w_hi, w_lo, rest, g_sem, a_sem, out_sem,
+    blocks, counts, listed, summed_in, tops_in, totals_in, q_hi_in, q_lo_in, k_in, m_in, v_in, w_hi_in, w_lo_in, feats, out,
+    summed, tops, totals, q_hi, q_lo, k_late, m_late, v_late, w_hi, w_lo, rest, g_sem, a_sem, out_sem,
 ):
     groups = blocks // 2
     rows = 2 * BLK
@@ -435,16 +440,16 @@
         refs = ((summed_in.at[i], summed.at[i]), (q_hi_in.at[i], q_hi.at[i]), (q_lo_in.at[i], q_lo.at[i]), (feats.at[group_rows(i)], rest.at[group_rows(i)]))
         return [pltpu.make_async_copy(*pair, g_sem.at[n, i]) for n, pair in enumerate(refs)]
 
-    refs = ((k_in, k_late), (v_in, v_late), (tops_in, tops), (totals_in, totals), (w_hi_in, w_hi), (w_lo_in, w_lo))
+    refs = ((k_in, k_late), (m_in, m_late), (v_in, v_late), (tops_in, tops), (totals_in, totals), (w_hi_in, w_hi), (w_lo_in, w_lo))
     shared = [pltpu.make_async_copy(*pair, a_sem.at[n]) for n, pair in enumerate(refs)]
 
     def out_copy(i):
         return pltpu.make_async_copy(rest.at[group_rows(i)], out.at[group_rows(i)], out_sem.at[i])
 
-    for copy in shared:
+    for copy in group_copies(0) + shared:
         copy.start()
 
-    @pl.loop(0, groups)
+    @pl.loop(1, groups)
     def _(i):
         for copy in group_copies(i):
             copy.start()
@@ -465,10 +470,14 @@
             @pl.when(pick >= 0)
             def _():
                 columns = pl.ds(pl.multiple_of(n * BLK, BLK), BLK)
+                lo = iota((BLK, PAIR), 1) < DIM
+                masks = m_late[pick].astype(F32)
 
                 def score(h):
                     here = slice(h * DIM, (h + 1) * DIM)
-                    return [dot(k_late[pick, h], queries_of(q_hi[i, here, columns], q_lo[i, here, columns]))]
+                    k = k_late[pick, h]
+                    again = jnp.where(lo, k.astype(F32), masks).astype(BF16)
+                    return [dot(jnp.concatenate([k, again], axis=1), queries_of(q_hi[i, here, columns], q_lo[i, here, columns]))]
 
                 def floor(h, _, top):
                     return jnp.maximum(top, tops[i, h, :, columns])
@@ -514,7 +523,7 @@
     rowed = (groups, HEADS, 8, 2 * BLK)
     shapes = [
         (wide, F32), (rowed, F32), (rowed, F32), (wide, BF16), (wide, BF16),
-        ((LATE + 1, HEADS, BLK, 2 * PAIR), BF16), ((LATE + 1, HEADS, PAIR, BLK), BF16),
+        ((LATE + 1, HEADS, BLK, PAIR), BF16), ((LATE + 1, BLK, PAIR), BF16), ((LATE + 1, HEADS, PAIR, BLK), BF16),
         ((width, width), BF16), ((width, width), BF16),
     ]
     middle = pl.pallas_call(
@@ -542,7 +551,7 @@
             pltpu.VMEM((groups, HEADS, 8, 2 * BLK), F32),
             dma((chunks,)), dma((chunks,)), dma((chunks,)), dma((chunks,)),
             dma((2,)), dma((2,)), dma((4,)), dma((4,)),
-            dma((groups,)), dma((8,)), dma((3, groups)), dma((2, groups)), dma((2, 2)), dma((2,)),
+            dma((groups,)), dma((8,)), dma((3, groups)), dma((2, groups)), dma((3, 2)), dma((2,)),
         ],
         compiler_params=pltpu.CompilerParams(
             collective_id=0, has_side_effects=True, vmem_limit_bytes=60 * 1024 * 1024
@@ -555,7 +564,7 @@
         in_specs=[smem, smem] + [hbm] * (len(shapes) + 1),
         out_specs=hbm,
         scratch_shapes=[pltpu.VMEM(*shape) for shape in shapes]
-        + [pltpu.VMEM((rows, width), F32), dma((4, groups)), dma((6,)), dma((groups,))],
+        + [pltpu.VMEM((rows, width), F32), dma((4, groups)), dma((7,)), dma((groups,))],
         compiler_params=pltpu.CompilerParams(vmem_limit_bytes=60 * 1024 * 1024),
     )(counts, cross_list[0].T, *middle, points)
     return mixed[None]

time: 133 us -> 133 us (level); the launches traced: 133 us -> 132 us
    pallas_call x1, Pallas kernels: 16.1 us -> 14.6 us  [body(): pl.pallas_call(functools.partial(finish_kernel, blocks), out_shape=jax.Sh...]
where the time goes in v7:
time: 133 us; the launch traced here: 132 us
  Pallas kernels  131 us (98%)
    pallas_call x1, Pallas kernels, body(): pl.pallas_call(functools.partial(kernel, blocks), out_shape=[jax.ShapeDty...  116 us
    pallas_call x1, Pallas kernels, body(): pl.pallas_call(functools.partial(finish_kernel, blocks), out_shape=jax.Sh...  14.6 us

profile of v7, /device:TPU:8, one launch (start us, length us, event | category | flops | bytes accessed | tf_op | source)
XLA Modules:
  0.0 131.6 jit_solution(8341313247877044907)
XLA Ops:
  0.7 116.2 %shard_map.73 = (f32[8,512,256]{2,1,0:T(8,128)}, f32[8,8,8,256]{3,2,1,0:T(8,128)}, f32[8,8,8,256]{3,2,1,0:T(8,128)}, bf16[8,512,256]{2,1,0:T(8,128)(2,1)}, bf16[...) custom-call(f32[2048,512]{1,0:T(8,128)} %bitcast.6, ...), custom_call_target="tpu_custom_call" | custom-call | tf_op jit(solution)/shard_map/pallas_call | solution.py:529
  116.9 14.6 %shard_map.74 = f32[2048,512]{1,0:T(8,128)} custom-call(s32[1,16]{1,0:T(1,128)} %counts.3, s32[2,16]{1,0:T(2,128)} %bitcast.9, f32[8,512,256]{2,1,0:T(8,128)} %get-tuple-element.15.summed_in, f32[8,8,8,256]{3,2,1,0:T(8,128)} %get-tuple-element.16.tops_in, f32[8,8,8,256]{3,2,1,0:T(8,128)} %get-tuple-element.17.totals_in, ...), custom_call_target="tpu_custom_call" | custom-call | tf_op jit(solution)/shard_map/pallas_call | solution.py:561
